TPU v7x, 32 devices: a whole 2x2x4 slice. The times are simulated.
32 devices in a mesh: lat: 16 (over z, y, x), wid: 2 (over core).
Axes of the slice: x: 2, y: 2, z: 4, core: 2. Of those that a mesh axis runs over, the one named last changes fastest.
Arguments:
- activations: bfloat16 [128, 3584], P(None, 'wid'), may hold values from -6 to 6
- encoder: bfloat16 [3584, 8192], P('wid', 'lat'), may hold values from -0.09375 to 0.09375
- encoder_bias: float32 [8192], P('lat'), may hold values from -3 to 3
- decoder: bfloat16 [8192, 3584], P('lat', 'wid'), may hold values from -0.75 to 0.75
- decoder_bias: float32 [3584], P('wid'), may hold values from -3 to 3
- kept_mask: int32 [128, 8192], P(None, 'lat'), may hold values 0 or 1
- boundaries: int32 [8], replicated, may hold values from 1025 to 8192, as said below
Outputs:
- encoder_grad: bfloat16 [3584, 8192], P('wid', 'lat')
- encoder_bias_grad: float32 [8192], P('lat')
- decoder_grad: bfloat16 [8192, 3584], P('lat', 'wid')
- decoder_bias_grad: float32 [3584], P('wid')
Inputs may be any that keep to these rules, and one draw needn't show every extreme that they name: `boundaries`: Rising; for k below 7, boundary k lies among the 512 latents that follow (k + 1) * 1024; the last equals 8192.
All inputs are finite; a program needn't handle non-finite values. No bound on the sum of `kept_mask` on one device may be relied on, other than what follows from the above.
Results may differ from a plain program's by a relative error of at most 0.006.
Values may be sent and summed in bfloat16 or wider, within the bound.
A program may use at most 128 MiB of HBM per device.

v0:
```python
import jax
import jax.numpy as jnp
from jax import lax
from jax.sharding import PartitionSpec as P

GROUPS = 8


def prefix(part, axis, combine, identity, reverse):
    count = lax.axis_size(axis)
    place = lax.axis_index(axis)
    ahead = count - 1 - place if reverse else place
    gathered = lax.all_gather(part, axis)
    state = jnp.zeros_like(part) + jnp.asarray(identity, part.dtype)

    def one(step, state):
        source = count - 1 - step if reverse else step
        return combine(state, lax.dynamic_index_in_dim(gathered, source, 0, False))

    return lax.fori_loop(0, ahead, one, state)


def add_terms(earlier, later):
    return earlier + later


def body(activations, encoder, encoder_bias, decoder, decoder_bias, kept_mask, boundaries):
    latent_width = encoder.shape[1]
    first_latent = lax.axis_index("lat") * latent_width
    latent_ids = first_latent + jnp.arange(latent_width, dtype=jnp.int32)
    kept_float = kept_mask.astype(jnp.float32)
    encoder_part = jnp.dot(activations, encoder, preferred_element_type=jnp.float32)
    preacts = lax.psum(encoder_part, "wid") + encoder_bias
    codes = (kept_float * preacts).astype(jnp.bfloat16)
    inside_rows = (boundaries > first_latent) & (boundaries <= first_latent + latent_width)
    holds_cut = jnp.any(inside_rows)
    cut_point = jnp.sum(jnp.where(inside_rows, boundaries, 0))
    below_cut = latent_ids < cut_point
    zero_code = jnp.zeros((), jnp.bfloat16)
    masked_codes = jnp.stack(
        [
            jnp.where(below_cut[None, :], codes, zero_code),
            jnp.where(below_cut[None, :], zero_code, codes),
        ]
    )
    decoded_pieces = jnp.einsum(
        "sbj,jd->sbd", masked_codes, decoder, preferred_element_type=jnp.float32
    )
    local_total = decoded_pieces[0] + decoded_pieces[1]
    zero_rows = jnp.zeros_like(local_total)
    prefix_sum = prefix(local_total, "lat", add_terms, zero_rows, False)
    target_rows = activations.astype(jnp.float32)
    scaled_error = jnp.where(
        holds_cut, (decoder_bias + prefix_sum + decoded_pieces[0] - target_rows) / GROUPS, 0.0
    )
    suffix_sum = prefix(scaled_error, "lat", add_terms, zero_rows, True)
    below_suffix = suffix_sum + scaled_error
    suffix_pair = jnp.stack([below_suffix, suffix_sum]).astype(jnp.bfloat16)
    back_grads = jnp.einsum("sbd,jd->sbj", suffix_pair, decoder, preferred_element_type=jnp.float32)
    partial_grads = jnp.where(below_cut[None, :], back_grads[0], back_grads[1])
    coded_grads = lax.psum(partial_grads, "wid")
    pre_grads = kept_float * coded_grads
    encoder_bias_grad = jnp.sum(pre_grads, axis=0)
    pre_low = pre_grads.astype(jnp.bfloat16)
    encoder_grad = lax.dot_general(
        activations, pre_low, (((0,), (0,)), ((), ())), preferred_element_type=jnp.float32
    ).astype(jnp.bfloat16)
    decoder_grad = jnp.einsum(
        "sbj,sbd->jd", masked_codes, suffix_pair, preferred_element_type=jnp.float32
    ).astype(jnp.bfloat16)
    decoder_bias_grad = lax.psum(jnp.sum(scaled_error, axis=0), "lat")
    return (encoder_grad, encoder_bias_grad, decoder_grad, decoder_bias_grad)


def solution(mesh):
    placed = (
        P(None, "wid"),
        P("wid", "lat"),
        P("lat"),
        P("lat", "wid"),
        P("wid"),
        P(None, "lat"),
        P(),
    )
    return jax.shard_map(
        body,
        mesh=mesh,
        in_specs=placed,
        out_specs=(P("wid", "lat"), P("lat"), P("lat", "wid"), P("wid")),
        check_vma=False,
    )
```

profile of v0, /device:TPU:0, one launch (start us, length us, event | category | flops | bytes accessed | tf_op | source)
XLA Modules:
  0.0 482.0 jit_solution(5879501251651244707)
XLA Ops:
  7.3 2.9 fusion.18
  11.5 20.4 %all-reduce.3.cloned.1.call-done = f32[128,512]{1,0:T(8,128)} async-done(((f32[128,512]{1,0:T(8,128)}), f32[128,512]{1,0:T(8,128)}) %all-reduce.3.cloned.1.call-update) | async-done | bytes 262160 | tf_op jit(solution)/shard_map/psum | solution.py:33
  31.9 1.0 select_bitcast_fusion.1
  33.7 1.2 copy-done.1
  34.9 1.0 slice_add_fusion
  36.7 172.5 %all-gather.4.cloned.1.call-done = f32[16,128,1792]{2,1,0:T(8,128)} async-done(((f32[1,128,1792]{2,1,0:T(8,128)}), f32[16,128,1792]{2,1,0:T(8,128)}) %all-gather.4.cloned.1.call-update) | async-done | bytes 14680080 | tf_op jit(solution)/shard_map/all_gather | solution.py:13
  209.3 1.0 copy-done.2
  210.2 2.9 fusion.16
  213.3 190.1 %all-gather.6.cloned.1.call-done = f32[2048,1792]{1,0:T(8,128)} async-done(((f32[128,1792]{1,0:T(8,128)}), f32[2048,1792]{1,0:T(8,128)}) %all-gather.6.cloned.1.call-update) | async-done | bytes 14680080 | tf_op jit(solution)/shard_map/all_gather | solution.py:13
  403.4 21.0 %while.23 = (s32[]{:T(128)}, f32[128,1792]{1,0:T(8,128)S(1)}, s32[]{:T(128)}, f32[16,128,1792]{2,1,0:T(8,128)}, s32[]{:T(128)}, /*index=5*/s32[]{:T(128)}, s32[]{:T(128)}, s32[]{:T(128)}) while((s32[]{:T(128)}, f32[128,1792]{1,0:T(8,128)S(1)}, s32[]{:T(128)}, f32[16,128,1792]{2,1,0:T(8,128)}, s32[]{:T(128)}, /*index=5*/s32[]{:T(128)}, ...), condition=%wide.region_6.7_spmd, body=%wide.region_5.6_spmd.sunk | while | flops 229382 | bytes 2752647 | solution.py:20
  403.5 1.4 bitcast_add_fusion.6
  404.9 1.4 bitcast_add_fusion.6
  406.3 1.4 bitcast_add_fusion.6
  407.7 1.4 bitcast_add_fusion.6
  409.1 1.4 bitcast_add_fusion.6
  410.5 1.4 bitcast_add_fusion.6
  411.8 1.4 bitcast_add_fusion.6
  413.2 1.4 bitcast_add_fusion.6
  414.6 1.4 bitcast_add_fusion.6
  416.0 1.4 bitcast_add_fusion.6
  417.4 1.4 bitcast_add_fusion.6
  418.8 1.4 bitcast_add_fusion.6
  420.2 1.4 bitcast_add_fusion.6
  421.6 1.4 bitcast_add_fusion.6
  423.0 1.4 bitcast_add_fusion.6
  424.4 1.3 fusion.8
  425.7 0.7 fusion.1
  426.6 0.7 fusion.9
  427.4 37.6 %psum.23 = f32[1792]{0:T(1024)} all-reduce(f32[1792]{0:T(1024)S(1)} %get-tuple-element.109), channel_id=1, replica_groups=mesh['lat'=16,'wid'=2] {'lat'}, use_global_device_ids=true, to_apply=%region_10.11 | all-reduce | flops 1792 | bytes 14336 | tf_op jit(solution)/shard_map/psum | solution.py:71
  465.0 3.1 bitcast_convert_fusion
  468.1 2.9 fusion
  471.0 3.9 copy.14
  (44 shorter events, 3.9 us)
Async XLA Ops:
  7.2 25.8 %copy-start = (bf16[512,1792]{1,0:T(8,128)(2,1)S(1)}, bf16[512,1792]{1,0:T(8,128)(2,1)}, u32[]{:S(2)}) copy-start(bf16[512,1792]{1,0:T(8,128)(2,1)} %param.14) | copy-start | bytes 5505028
  7.2 3.0 copy-start.13
  7.2 24.8 %copy-start.12 = (f32[512]{0:T(512)S(1)}, f32[512]{0:T(512)}, u32[]{:S(2)}) copy-start(f32[512]{0:T(512)} %param.13) | copy-start | bytes 6148
  7.2 24.7 %copy-start.3 = (s32[128,512]{1,0:T(8,128)S(1)}, s32[128,512]{1,0:T(8,128)}, u32[]{:S(2)}) copy-start(s32[128,512]{1,0:T(8,128)} %param.16) | copy-start | bytes 786436
  7.2 24.7 %all-reduce.3.cloned.1.call-start = ((), (), s32[]{:S(2)}) async-start(), calls=%async_computation | async-start | bytes 524288 | tf_op jit(solution)/shard_map/psum | solution.py:33
  10.2 199.0 %all-gather.4.cloned.1.call-start = ((), (), s32[]{:S(2)}) async-start(), calls=%async_computation.1 | async-start | bytes 15597568 | tf_op jit(solution)/shard_map/all_gather | solution.py:13
  33.0 0.7 copy-start.7
  33.0 0.7 copy-start.5
  33.7 1.2 copy-start.1
  36.0 367.4 %all-gather.6.cloned.1.call-start = ((), (), s32[]{:S(2)}) async-start(), calls=%async_computation.3 | async-start | bytes 15597568 | tf_op jit(solution)/shard_map/all_gather | solution.py:13
  209.2 1.0 copy-start.2
  209.2 1.0 copy-start.11
  213.2 254.9 %all-reduce.5.cloned.1.call-start = ((), (), s32[]{:S(2)}) async-start(), calls=%async_computation.2 | async-start | bytes 524288 | tf_op jit(solution)/shard_map/psum | solution.py:61
  425.7 0.8 copy-start.9
  425.7 0.9 copy-start.10
  425.7 39.3 %copy-start.6 = (bf16[1,128,512]{2,1,0:T(8,128)(2,1)S(1)}, bf16[1,128,512]{2,1,0:T(8,128)(2,1)}, u32[]{:S(2)}) copy-start(bf16[1,128,512]{2,1,0:T(8,128)(2,1)} %copy-done.5) | copy-start | bytes 393220
  425.7 39.3 %copy-start.8 = (bf16[1,128,512]{2,1,0:T(8,128)(2,1)S(1)}, bf16[1,128,512]{2,1,0:T(8,128)(2,1)}, u32[]{:S(2)}) copy-start(bf16[1,128,512]{2,1,0:T(8,128)(2,1)} %copy-done.7) | copy-start | bytes 393220
  471.0 3.9 copy-start.4
Sparse Core Ops, SparseCore 0:
  10.9 20.9 all-reduce.2
  36.1 173.0 all-gather.3
  213.3 189.9 all-gather.5
  427.5 14.1 all-reduce.4
where the time goes:
time: 483 us; the launch traced here: 482 us
  waiting for transfers between devices  383 us (79%)
  blocking collectives  37.6 us (8%)
  other arithmetic  30.1 us (6%)
  between operations  14 us (3%)
  matrix products  10.2 us (2%)
  local copies, waits for them, and re-layouts  6.45 us (1%)
    all_gather x2, waiting for transfers between devices, prefix(): gathered = lax.all_gather(part, axis)  363 us
    psum x1, blocking collectives, body(): decoder_bias_grad = lax.psum(jnp.sum(scaled_error, axis=0), 'lat')  37.6 us
    add x15, other arithmetic, add_terms(): return earlier + later  20.6 us
    psum x1, waiting for transfers between devices, body(): preacts = lax.psum(encoder_part, 'wid') + encoder_bias  20.4 us
  transfers between devices with their start and end apart: 4, of which 3 were waited for; matrix products, arithmetic and copies ran while one was open for 1% of the time, Pallas kernels for 0%

commit v1 on v0

--- a/solution.py
+++ b/solution.py
@@ -1,9 +1,17 @@
+import functools
+
 import jax
 import jax.numpy as jnp
 from jax import lax
+from jax.experimental import pallas as pl
+from jax.experimental.pallas import tpu as pltpu
 from jax.sharding import PartitionSpec as P
 
 GROUPS = 8
+HALF = 8
+SUB = 16
+CHUNKS = 2
+MESH = pl.DeviceIdType.MESH
 
 
 def prefix(part, axis, combine, identity, reverse):
@@ -24,7 +32,7 @@
     return earlier + later
 
 
-def body(activations, encoder, encoder_bias, decoder, decoder_bias, kept_mask, boundaries):
+def general_body(activations, encoder, encoder_bias, decoder, decoder_bias, kept_mask, boundaries):
     latent_width = encoder.shape[1]
     first_latent = lax.axis_index("lat") * latent_width
     latent_ids = first_latent + jnp.arange(latent_width, dtype=jnp.int32)
@@ -72,6 +80,395 @@
     return (encoder_grad, encoder_bias_grad, decoder_grad, decoder_bias_grad)
 
 
+def reduce_pieces(pieces, chunk):
+    def piece(source, which):
+        return pieces[chunk, source, which].astype(jnp.float32)
+
+    upper = [piece(2 * k, 1) + piece(2 * k + 1, 1) for k in range(4)]
+    lower = [piece(2 * k, 0) for k in range(4)]
+    segments = [upper[k] + lower[k + 1] for k in range(3)] + [upper[3]]
+    return lower[0], segments
+
+
+def exchange_kernel(
+    act_hbm, enc_hbm, enc_bias, dec_hbm, dec_bias, mask_hbm, bounds,
+    codes_out, suffix_out, pre_out, enc_bias_out, dec_bias_out,
+    act, enc, dec, mask, part, part_in, grad, grad_in, codes,
+    pieces_out, pieces, cross_out, cross_in, tails, suffix,
+    row_out, rows, final_out, final_in,
+    load_sems, wid_sems, a_send, a_recv, x_send, x_recv, b_send, b_recv, r_send, r_recv, store_sems,
+):
+    lat = lax.axis_index("lat")
+    wid = lax.axis_index("wid")
+    half = lat // HALF
+    place = lat % HALF
+    even = place % 2 == 0
+    odd = place % 2 == 1
+    width = act.shape[1]
+    wide = width // CHUNKS
+    block = dec.shape[0]
+    other_core = {"lat": lat, "wid": 1 - wid}
+    other_half = {"lat": (lat + HALF) % (2 * HALF), "wid": wid}
+
+    def peer(step):
+        return (place + step) % HALF
+
+    def source(step):
+        return (place + HALF - step) % HALF
+
+    def device(position):
+        return {"lat": half * HALF + position, "wid": wid}
+
+    def remote(src, dst, send, recv, target):
+        return pltpu.make_async_remote_copy(
+            src_ref=src, dst_ref=dst, send_sem=send, recv_sem=recv, device_id=target, device_id_type=MESH
+        )
+
+    barrier = pltpu.get_barrier_semaphore()
+    for step in range(1, HALF):
+        pl.semaphore_signal(barrier, inc=1, device_id=device(peer(step)), device_id_type=MESH)
+    pl.semaphore_signal(barrier, inc=1, device_id=other_core, device_id_type=MESH)
+    pl.semaphore_signal(barrier, inc=1, device_id=other_half, device_id_type=MESH)
+
+    load_act = pltpu.make_async_copy(act_hbm, act, load_sems.at[0])
+    load_act.start()
+    load_enc = []
+    for c in range(CHUNKS):
+        span = pl.ds(c * wide, wide)
+        load_enc.append(pltpu.make_async_copy(enc_hbm.at[span], enc.at[span], load_sems.at[1 + c]))
+        load_enc[-1].start()
+    load_mask = pltpu.make_async_copy(mask_hbm, mask, load_sems.at[1 + CHUNKS])
+    load_mask.start()
+    load_dec = pltpu.make_async_copy(dec_hbm, dec, load_sems.at[2 + CHUNKS])
+    load_dec.start()
+
+    @pl.when(odd)
+    def _():
+        for c in range(CHUNKS):
+            for r in range(HALF):
+                suffix[c, r, 0] = jnp.zeros((SUB, wide), jnp.bfloat16)
+
+    load_act.wait()
+    total = None
+    for c in range(CHUNKS):
+        load_enc[c].wait()
+        term = jnp.dot(
+            act[:, c * wide : (c + 1) * wide], enc[c * wide : (c + 1) * wide, :], preferred_element_type=jnp.float32
+        )
+        total = term if total is None else total + term
+    part[...] = total
+    pl.semaphore_wait(barrier, HALF + 1)
+    swap = remote(part, part_in, wid_sems.at[0], wid_sems.at[1], other_core)
+    swap.start()
+
+    first = lat * block
+    cut = jnp.int32(0)
+    for k in range(GROUPS - 1):
+        bound = bounds[k]
+        cut = cut + jnp.where((bound > first) & (bound <= first + block), bound, 0)
+    tokens = act.shape[0]
+    below = (lax.broadcasted_iota(jnp.int32, (tokens, block), 1) + first) < cut
+    load_mask.wait()
+    kept = mask[...].astype(jnp.float32)
+    load_dec.wait()
+    swap.wait()
+    full = kept * ((part[...] + part_in[...]) + enc_bias[...])
+    low = jnp.where(below, full, 0.0).astype(jnp.bfloat16)
+    high = jnp.where(below, 0.0, full).astype(jnp.bfloat16)
+    for r in range(HALF):
+        codes[2 * SUB * r : 2 * SUB * r + SUB, :] = low[SUB * r : SUB * (r + 1), :]
+        codes[2 * SUB * r + SUB : 2 * SUB * (r + 1), :] = high[SUB * r : SUB * (r + 1), :]
+    store_codes = pltpu.make_async_copy(codes, codes_out, store_sems.at[0])
+    store_codes.start()
+
+    def send_pieces(c, step, both):
+        target = peer(step)
+        if both:
+            src, dst = pieces_out.at[c, target], pieces.at[c, place]
+        else:
+            src, dst = pieces_out.at[c, target, 1], pieces.at[c, place, 1]
+        return remote(src, dst, a_send.at[c, step], a_recv.at[c, place], device(target))
+
+    def wait_pieces(c, step):
+        origin = source(step)
+
+        @pl.when(origin % 2 == 0)
+        def _():
+            remote(
+                pieces_out.at[c, origin], pieces.at[c, origin], a_send.at[c, step], a_recv.at[c, origin], device(origin)
+            ).wait_recv()
+
+        @pl.when(origin % 2 == 1)
+        def _():
+            remote(
+                pieces_out.at[c, origin, 1], pieces.at[c, origin, 1], a_send.at[c, step], a_recv.at[c, origin],
+                device(origin),
+            ).wait_recv()
+
+    for c in range(CHUNKS):
+        made = jnp.dot(codes[...], dec[:, c * wide : (c + 1) * wide], preferred_element_type=jnp.float32)
+        pieces_out[c] = made.astype(jnp.bfloat16).reshape(HALF, 2, SUB, wide)
+
+        @pl.when(even)
+        def _():
+            for step in range(1, HALF):
+                send_pieces(c, step, True).start()
+
+        @pl.when(odd)
+        def _():
+            for step in range(1, HALF):
+                send_pieces(c, step, False).start()
+
+        pieces[c, place] = pieces_out[c, place]
+
+    crossing = []
+    for c in range(CHUNKS):
+        for step in range(1, HALF):
+            wait_pieces(c, step)
+        low0, seg = reduce_pieces(pieces, c)
+        plain = ((low0 + seg[0]) + seg[1]) + (seg[2] + seg[3])
+        weighted = ((5.0 * low0 + 4.0 * seg[0]) + 3.0 * seg[1]) + (2.0 * seg[2] + seg[3])
+        cross_out[c] = jnp.where(half == 0, plain, weighted).astype(jnp.bfloat16)
+        crossing.append(remote(cross_out.at[c], cross_in.at[c], x_send.at[c], x_recv.at[c], other_half))
+        crossing[-1].start()
+
+    def send_suffix(c, step, both):
+        target = peer(step)
+        if both:
+            src, dst = tails.at[c, pl.ds(target // 2, 2)], suffix.at[c, place]
+        else:
+            src, dst = tails.at[c, target // 2 + 1], suffix.at[c, place, 1]
+        return remote(src, dst, b_send.at[c, step], b_recv.at[c, place], device(target))
+
+    later = half.astype(jnp.float32)
+    own_rows = pl.ds(pl.multiple_of(place * SUB, SUB), SUB)
+    for c in range(CHUNKS):
+        span = slice(c * wide, (c + 1) * wide)
+        low0, seg = reduce_pieces(pieces, c)
+        crossing[c].wait_recv()
+        got = cross_in[c].astype(jnp.float32)
+        base = dec_bias[:, span] - act[own_rows, span].astype(jnp.float32)
+        before = base + later * (got + low0)
+        errors = []
+        running = before
+        for k in range(4):
+            running = running + seg[k]
+            errors.append(running)
+        tail = jnp.where(half == 0, 5.0 * errors[3] + got, errors[3])
+        scaled = [tail]
+        for k in (2, 1, 0):
+            tail = tail + errors[k]
+            scaled.append(tail)
+        scaled.append(tail + before)
+        for k in range(5):
+            tails[c, k] = (scaled[4 - k] / GROUPS).astype(jnp.bfloat16)
+        row_out[:, span] = jnp.sum(scaled[3] / GROUPS, axis=0, keepdims=True)
+        for step in range(1, HALF):
+
+            @pl.when(peer(step) % 2 == 0)
+            def _():
+                send_suffix(c, step, True).start()
+
+            @pl.when(peer(step) % 2 == 1)
+            def _():
+                send_suffix(c, step, False).start()
+
+        suffix[c, place] = tails[c, pl.ds(place // 2, 2)]
+
+    def row_copy(step):
+        return remote(row_out, rows.at[place], r_send.at[step], r_recv.at[place], device(peer(step)))
+
+    for step in range(1, HALF):
+        row_copy(step).start()
+    rows[place] = row_out[...]
+
+    back = None
+    stores = []
+    for c in range(CHUNKS):
+
+        @pl.when(even)
+        def _():
+            for step in range(1, HALF):
+                origin = source(step)
+                remote(
+                    suffix.at[c, origin], suffix.at[c, origin], b_send.at[c, step], b_recv.at[c, origin], device(origin)
+                ).wait_recv()
+
+        @pl.when(odd)
+        def _():
+            for step in range(1, HALF):
+                origin = source(step)
+                remote(
+                    suffix.at[c, origin, 1], suffix.at[c, origin, 1], b_send.at[c, step], b_recv.at[c, origin],
+                    device(origin),
+                ).wait_recv()
+
+        stores.append(pltpu.make_async_copy(suffix.at[c], suffix_out.at[c], store_sems.at[1 + c]))
+        stores[-1].start()
+        term = lax.dot_general(
+            suffix[c].reshape(2 * tokens, wide), dec[:, c * wide : (c + 1) * wide],
+            (((1,), (1,)), ((), ())), preferred_element_type=jnp.float32,
+        )
+        back = term if back is None else back + term
+    pair = back.reshape(HALF, 2, SUB, block)
+    below_parts = below.astype(jnp.float32).reshape(HALF, SUB, block) > 0.5
+    grad[...] = jnp.where(below_parts, pair[:, 0], pair[:, 1]).reshape(tokens, block)
+    swap_back = remote(grad, grad_in, wid_sems.at[2], wid_sems.at[3], other_core)
+    swap_back.start()
+
+    for step in range(1, HALF):
+        origin = source(step)
+        remote(row_out, rows.at[origin], r_send.at[step], r_recv.at[origin], device(origin)).wait_recv()
+    summed = rows[0]
+    for r in range(1, HALF):
+        summed = summed + rows[r]
+    final_out[...] = summed
+    finish = remote(final_out, final_in, x_send.at[CHUNKS], x_recv.at[CHUNKS], other_half)
+    finish.start()
+
+    swap_back.wait()
+    pre = kept * (grad[...] + grad_in[...])
+    enc_bias_out[...] = jnp.sum(pre, axis=0, keepdims=True)
+    pre_out[...] = pre.astype(jnp.bfloat16)
+
+    for c in range(CHUNKS):
+        crossing[c].wait_send()
+
+        @pl.when(even)
+        def _():
+            for step in range(1, HALF):
+                send_pieces(c, step, True).wait_send()
+
+        @pl.when(odd)
+        def _():
+            for step in range(1, HALF):
+                send_pieces(c, step, False).wait_send()
+
+        for step in range(1, HALF):
+
+            @pl.when(peer(step) % 2 == 0)
+            def _():
+                send_suffix(c, step, True).wait_send()
+
+            @pl.when(peer(step) % 2 == 1)
+            def _():
+                send_suffix(c, step, False).wait_send()
+
+    for step in range(1, HALF):
+        row_copy(step).wait_send()
+    finish.wait()
+    dec_bias_out[...] = jnp.where(half == 0, final_out[...], final_in[...])
+    store_codes.wait()
+    for store in stores:
+        store.wait()
+
+
+def grads_kernel(act, pre, codes, suffix, enc_bias_in, dec_bias_in, enc_grad, dec_grad, enc_bias_out, dec_bias_out):
+    contract_rows = (((0,), (0,)), ((), ()))
+    enc_grad[...] = lax.dot_general(act[...], pre[...], contract_rows, preferred_element_type=jnp.float32).astype(
+        jnp.bfloat16
+    )
+    dec_grad[...] = lax.dot_general(
+        codes[...], suffix[0], contract_rows, preferred_element_type=jnp.float32
+    ).astype(jnp.bfloat16)
+    enc_bias_out[...] = enc_bias_in[...]
+    dec_bias_out[...] = dec_bias_in[...]
+
+
+def kernel_body(activations, encoder, encoder_bias, decoder, decoder_bias, kept_mask, boundaries):
+    tokens, width = activations.shape
+    block = encoder.shape[1]
+    wide = width // CHUNKS
+    low, full = jnp.bfloat16, jnp.float32
+    hbm = pl.BlockSpec(memory_space=pl.ANY)
+    vmem = pl.BlockSpec(memory_space=pltpu.VMEM)
+    smem = pl.BlockSpec(memory_space=pltpu.SMEM)
+    dma = pltpu.SemaphoreType.DMA
+    codes, suffix, pre, enc_bias_grad, dec_bias_grad = pl.pallas_call(
+        exchange_kernel,
+        out_shape=[
+            jax.ShapeDtypeStruct((2 * tokens, block), low),
+            jax.ShapeDtypeStruct((CHUNKS, HALF, 2, SUB, wide), low),
+            jax.ShapeDtypeStruct((tokens, block), low),
+            jax.ShapeDtypeStruct((1, block), full),
+            jax.ShapeDtypeStruct((1, width), full),
+        ],
+        in_specs=[hbm, hbm, vmem, hbm, vmem, hbm, smem],
+        out_specs=[hbm, hbm, vmem, vmem, vmem],
+        scratch_shapes=[
+            pltpu.VMEM((tokens, width), low),
+            pltpu.VMEM((width, block), low),
+            pltpu.VMEM((block, width), low),
+            pltpu.VMEM((tokens, block), jnp.int32),
+            pltpu.VMEM((tokens, block), full),
+            pltpu.VMEM((tokens, block), full),
+            pltpu.VMEM((tokens, block), full),
+            pltpu.VMEM((tokens, block), full),
+            pltpu.VMEM((2 * tokens, block), low),
+            pltpu.VMEM((CHUNKS, HALF, 2, SUB, wide), low),
+            pltpu.VMEM((CHUNKS, HALF, 2, SUB, wide), low),
+            pltpu.VMEM((CHUNKS, SUB, wide), low),
+            pltpu.VMEM((CHUNKS, SUB, wide), low),
+            pltpu.VMEM((CHUNKS, 5, SUB, wide), low),
+            pltpu.VMEM((CHUNKS, HALF, 2, SUB, wide), low),
+            pltpu.VMEM((1, width), full),
+            pltpu.VMEM((HALF, 1, width), full),
+            pltpu.VMEM((1, width), full),
+            pltpu.VMEM((1, width), full),
+            dma((3 + CHUNKS,)),
+            dma((4,)),
+            dma((CHUNKS, HALF)),
+            dma((CHUNKS, HALF)),
+            dma((CHUNKS + 1,)),
+            dma((CHUNKS + 1,)),
+            dma((CHUNKS, HALF)),
+            dma((CHUNKS, HALF)),
+            dma((HALF,)),
+            dma((HALF,)),
+            dma((1 + CHUNKS,)),
+        ],
+        compiler_params=pltpu.CompilerParams(
+            collective_id=0, has_side_effects=True, vmem_limit_bytes=40 * 1024 * 1024
+        ),
+        name="exchange",
+    )(
+        activations, encoder, encoder_bias.reshape(1, block), decoder, decoder_bias.reshape(1, width), kept_mask,
+        boundaries,
+    )
+    suffix = suffix.reshape(CHUNKS, 2 * tokens, wide)
+    enc_grad, dec_grad, enc_bias_grad, dec_bias_grad = pl.pallas_call(
+        grads_kernel,
+        grid=(CHUNKS,),
+        out_shape=[
+            jax.ShapeDtypeStruct((width, block), low),
+            jax.ShapeDtypeStruct((block, width), low),
+            jax.ShapeDtypeStruct((1, block), full),
+            jax.ShapeDtypeStruct((1, width), full),
+        ],
+        in_specs=[
+            pl.BlockSpec((tokens, wide), lambda c: (0, c)),
+            pl.BlockSpec((tokens, block), lambda c: (0, 0)),
+            pl.BlockSpec((2 * tokens, block), lambda c: (0, 0)),
+            pl.BlockSpec((1, 2 * tokens, wide), lambda c: (c, 0, 0)),
+            pl.BlockSpec((1, block), lambda c: (0, 0)),
+            pl.BlockSpec((1, width), lambda c: (0, 0)),
+        ],
+        out_specs=[
+            pl.BlockSpec((wide, block), lambda c: (c, 0)),
+            pl.BlockSpec((block, wide), lambda c: (0, c)),
+            pl.BlockSpec((1, block), lambda c: (0, 0)),
+            pl.BlockSpec((1, width), lambda c: (0, 0)),
+        ],
+        compiler_params=pltpu.CompilerParams(vmem_limit_bytes=32 * 1024 * 1024),
+        name="grads",
+    )(activations, pre, codes, suffix, enc_bias_grad, dec_bias_grad)
+    return enc_grad, enc_bias_grad.reshape(block), dec_grad, dec_bias_grad.reshape(width)
+
+
+def fits(mesh):
+    return mesh.shape["lat"] == 2 * HALF and mesh.shape["wid"] == 2
+
+
 def solution(mesh):
     placed = (
         P(None, "wid"),
@@ -83,7 +480,7 @@
         P(),
     )
     return jax.shard_map(
-        body,
+        kernel_body if fits(mesh) else general_body,
         mesh=mesh,
         in_specs=placed,
         out_specs=(P("wid", "lat"), P("lat"), P("lat", "wid"), P("wid")),

time: 483 us -> 48.5 us (0.10)
  waiting for transfers between devices: 383 us -> 0 us
  Pallas kernels: 0 us -> 39.9 us
  blocking collectives: 37.6 us -> 0 us
  other arithmetic: 30.1 us -> 0.62 us
  between operations: 14 us -> 0.65 us
  matrix products: 10.2 us -> 0 us
    all_gather x2 -> x0, waiting for transfers between devices: 363 us -> none  [prefix(): gathered = lax.all_gather(part, axis)]
    pallas_call x0 -> x2, Pallas kernels: none -> 39.9 us  [the longest x1 37.4 us: kernel_body(): pl.pallas_call(exchange_kernel, out_shape=[jax.ShapeDtypeStruct((2 * toke...]
    psum x1 -> x0, blocking collectives: 37.6 us -> none  [body(): decoder_bias_grad = lax.psum(jnp.sum(scaled_error, axis=0), 'lat')]
    add x16 -> x0, other arithmetic: 21.6 us -> none  [the longest x15 20.6 us: add_terms(): return earlier + later]
    psum x2 -> x0, waiting for transfers between devices: 20.4 us -> none  [the longest x1 20.4 us: body(): preacts = lax.psum(encoder_part, 'wid') + encoder_bias]
    dot_general x5 -> x0, matrix products: 10.2 us -> none  [the longest x1 3.07 us: body(): jnp.einsum('sbj,sbd->jd', masked_codes, suffix_pair, preferred_element_ty...]
  transfers between devices with their start and end apart: 4 -> 0, of which waited for: 3 -> 0; matrix products, arithmetic and copies ran while one was open for 1% -> 0% of each run, Pallas kernels for 0% -> 0%
where the time goes in v1:
time: 48.5 us; the launch traced here: 48.2 us
  Pallas kernels  39.9 us (82%)
  local copies, waits for them, and re-layouts  7 us (14%)
  between operations  0.65 us (1%)
  other arithmetic  0.62 us (1%)
    pallas_call x1, Pallas kernels, kernel_body(): pl.pallas_call(exchange_kernel, out_shape=[jax.ShapeDtypeStruct((2 * toke...  37.4 us
    unnamed x12, local copies, waits for them, and re-layouts  6.3 us
    pallas_call x1, Pallas kernels, kernel_body(): pl.pallas_call(grads_kernel, grid=(CHUNKS,), out_shape=[jax.ShapeDtypeStr...  2.44 us

profile of v1, /device:TPU:0, one launch (start us, length us, event | category | flops | bytes accessed | tf_op | source)
XLA Modules:
  0.0 48.2 jit_solution(1873453289372720268)
XLA Ops:
  0.6 0.7 %reshape.24.dec_bias = f32[1,1792]{1,0:T(1,128)S(1)} reshape(f32[1792]{0:T(1024)} %param.11) | data formatting | bytes 14336 | tf_op jit(solution)/shard_map/reshape | solution.py:435
  1.3 0.0 copy-start
  1.3 1.0 %copy-done = bf16[128,1792]{1,0:T(8,128)(2,1)S(1)} copy-done((bf16[128,1792]{1,0:T(8,128)(2,1)S(1)}, bf16[128,1792]{1,0:T(8,128)(2,1)}, u32[]{:S(2)}) %copy-start) | copy-done | bytes 458776
  2.4 0.0 copy-start.1
  2.4 1.5 %copy-done.1 = bf16[1792,512]{1,0:T(8,128)(2,1)S(1)} copy-done((bf16[1792,512]{1,0:T(8,128)(2,1)S(1)}, bf16[1792,512]{1,0:T(8,128)(2,1)}, u32[]{:S(2)}) %copy-start.1) | copy-done | bytes 1835032
  3.9 0.0 copy-start.2
  3.9 1.5 %copy-done.2 = bf16[512,1792]{1,0:T(8,128)(2,1)S(1)} copy-done((bf16[512,1792]{1,0:T(8,128)(2,1)S(1)}, bf16[512,1792]{1,0:T(8,128)(2,1)}, u32[]{:S(2)}) %copy-start.2) | copy-done | bytes 1835032
  5.4 0.0 copy-start.3
  5.4 0.9 %copy-done.3 = s32[128,512]{1,0:T(8,128)S(1)} copy-done((s32[128,512]{1,0:T(8,128)S(1)}, s32[128,512]{1,0:T(8,128)}, u32[]{:S(2)}) %copy-start.3) | copy-done | bytes 262168
  6.3 0.0 copy-start.4
  6.3 0.7 %copy-done.4 = f32[512]{0:T(512)S(1)} copy-done((f32[512]{0:T(512)S(1)}, f32[512]{0:T(512)}, u32[]{:S(2)}) %copy-start.4) | copy-done | bytes 2072
  7.0 0.0 copy-start.5
  7.0 0.7 %copy-done.5 = s32[8]{0:T(128)S(1)} copy-done((s32[8]{0:T(128)S(1)}, s32[8]{0:T(128)}, u32[]{:S(2)}) %copy-start.5) | copy-done | bytes 56
  7.6 37.4 %exchange.1 = (bf16[256,512]{1,0:T(8,128)(2,1)S(1)}, bf16[2,8,2,16,896]{4,3,2,1,0:T(8,128)(2,1)S(1)}, bf16[128,512]{1,0:T(8,128)(2,1)S(1)}, f32[1,512]{1,0:T(1,128)S(1)}, f32[1,1792]{1,0:T(1,128)S(1)}) custom-call(bf16[128,1792]{1,0:T(8,128)(2,1)S(1)} %copy-done, bf16[1792,512]{1,0:T(8,128)(2,1)S(1)} %copy-done.1, f32[1,512]{1,0:T(1,128)S(1)} %bitcast.4, ...), custom_call_target="tpu_custom_call" | custom-call | tf_op jit(solution)/shard_map/exchange/pallas_call | solution.py:387
  45.1 2.4 %grads.1 = (bf16[1792,512]{1,0:T(8,128)(2,1)}, bf16[512,1792]{1,0:T(8,128)(2,1)}, f32[1,512]{1,0:T(1,128)}, f32[1,1792]{1,0:T(1,128)S(1)}) custom-call(bf16[128,1792]{1,0:T(8,128)(2,1)S(1)} %copy-done, bf16[128,512]{1,0:T(8,128)(2,1)S(1)} %get-tuple-element.13.pre, bf16[256,512]{1,0:T(8,128)(2,1)S(1)} %get-tuple-element.14.codes, ...), custom_call_target="tpu_custom_call" | custom-call | tf_op jit(solution)/shard_map/grads/pallas_call | solution.py:439
  47.5 0.6 %reduce = f32[1792]{0:T(1024)} reduce(f32[1,1792]{1,0:T(1,128)S(1)} %get-tuple-element.21, f32[]{:T(128)} %constant), dimensions={0}, to_apply=%get-tuple-element.21.reduce_sub_computation | reduce | bytes 14340 | tf_op jit(solution)/shard_map/grads/pallas_call | solution.py:439
Async XLA Ops:
  1.3 1.0 %copy-start = (bf16[128,1792]{1,0:T(8,128)(2,1)S(1)}, bf16[128,1792]{1,0:T(8,128)(2,1)}, u32[]{:S(2)}) copy-start(bf16[128,1792]{1,0:T(8,128)(2,1)} %act.1) | copy-start | bytes 1376260
  2.4 1.5 %copy-start.1 = (bf16[1792,512]{1,0:T(8,128)(2,1)S(1)}, bf16[1792,512]{1,0:T(8,128)(2,1)}, u32[]{:S(2)}) copy-start(bf16[1792,512]{1,0:T(8,128)(2,1)} %enc_hbm.1) | copy-start | bytes 5505028
  3.9 1.5 %copy-start.2 = (bf16[512,1792]{1,0:T(8,128)(2,1)S(1)}, bf16[512,1792]{1,0:T(8,128)(2,1)}, u32[]{:S(2)}) copy-start(bf16[512,1792]{1,0:T(8,128)(2,1)} %dec_hbm.1) | copy-start | bytes 5505028
  5.4 0.9 %copy-start.3 = (s32[128,512]{1,0:T(8,128)S(1)}, s32[128,512]{1,0:T(8,128)}, u32[]{:S(2)}) copy-start(s32[128,512]{1,0:T(8,128)} %mask_hbm.1) | copy-start | bytes 786436
  6.3 0.7 %copy-start.4 = (f32[512]{0:T(512)S(1)}, f32[512]{0:T(512)}, u32[]{:S(2)}) copy-start(f32[512]{0:T(512)} %param.9) | copy-start | bytes 6148
  7.0 0.7 %copy-start.5 = (s32[8]{0:T(128)S(1)}, s32[8]{0:T(128)}, u32[]{:S(2)}) copy-start(s32[8]{0:T(128)} %bounds.1) | copy-start | bytes 100

commit v2 on v1

--- a/solution.py
+++ b/solution.py
@@ -10,7 +10,8 @@
 GROUPS = 8
 HALF = 8
 SUB = 16
-CHUNKS = 2
+LANES = 128
+STEPS = 2
 MESH = pl.DeviceIdType.MESH
 
 
@@ -80,9 +81,19 @@
     return (encoder_grad, encoder_bias_grad, decoder_grad, decoder_bias_grad)
 
 
-def reduce_pieces(pieces, chunk):
+def column_chunks(width):
+    tiles = width // LANES
+    widths = []
+    while tiles > 0:
+        widths.append(min(2 if not widths else 4, tiles))
+        tiles -= widths[-1]
+    ends = [LANES * sum(widths[: k + 1]) for k in range(len(widths))]
+    return [slice(end - LANES * count, end) for end, count in zip(ends, widths)]
+
+
+def reduce_pieces(pieces, span):
     def piece(source, which):
-        return pieces[chunk, source, which].astype(jnp.float32)
+        return pieces[source, which, :, span].astype(jnp.float32)
 
     upper = [piece(2 * k, 1) + piece(2 * k + 1, 1) for k in range(4)]
     lower = [piece(2 * k, 0) for k in range(4)]
@@ -91,9 +102,9 @@
 
 
 def exchange_kernel(
-    act_hbm, enc_hbm, enc_bias, dec_hbm, dec_bias, mask_hbm, bounds,
+    act_hbm, enc_hbm, enc_bias_hbm, dec_hbm, dec_bias_hbm, mask_hbm, bounds,
     codes_out, suffix_out, pre_out, enc_bias_out, dec_bias_out,
-    act, enc, dec, mask, part, part_in, grad, grad_in, codes,
+    act, enc, enc_bias, dec, dec_bias, mask, part, part_in, grad, grad_in, codes,
     pieces_out, pieces, cross_out, cross_in, tails, suffix,
     row_out, rows, final_out, final_in,
     load_sems, wid_sems, a_send, a_recv, x_send, x_recv, b_send, b_recv, r_send, r_recv, store_sems,
@@ -105,7 +116,9 @@
     even = place % 2 == 0
     odd = place % 2 == 1
     width = act.shape[1]
-    wide = width // CHUNKS
+    spans = column_chunks(width)
+    chunks = len(spans)
+    views = [pl.ds(span.start, span.stop - span.start) for span in spans]
     block = dec.shape[0]
     other_core = {"lat": lat, "wid": 1 - wid}
     other_half = {"lat": (lat + HALF) % (2 * HALF), "wid": wid}
@@ -133,28 +146,30 @@
     load_act = pltpu.make_async_copy(act_hbm, act, load_sems.at[0])
     load_act.start()
     load_enc = []
-    for c in range(CHUNKS):
-        span = pl.ds(c * wide, wide)
-        load_enc.append(pltpu.make_async_copy(enc_hbm.at[span], enc.at[span], load_sems.at[1 + c]))
+    for c in range(2):
+        rows_of = pl.ds(c * (width // 2), width // 2)
+        load_enc.append(pltpu.make_async_copy(enc_hbm.at[rows_of], enc.at[rows_of], load_sems.at[1 + c]))
         load_enc[-1].start()
-    load_mask = pltpu.make_async_copy(mask_hbm, mask, load_sems.at[1 + CHUNKS])
+    load_mask = pltpu.make_async_copy(mask_hbm, mask, load_sems.at[3])
     load_mask.start()
-    load_dec = pltpu.make_async_copy(dec_hbm, dec, load_sems.at[2 + CHUNKS])
+    load_enc_bias = pltpu.make_async_copy(enc_bias_hbm, enc_bias.at[0], load_sems.at[4])
+    load_enc_bias.start()
+    load_dec = pltpu.make_async_copy(dec_hbm, dec, load_sems.at[5])
     load_dec.start()
+    load_dec_bias = pltpu.make_async_copy(dec_bias_hbm, dec_bias.at[0], load_sems.at[6])
+    load_dec_bias.start()
 
     @pl.when(odd)
     def _():
-        for c in range(CHUNKS):
-            for r in range(HALF):
-                suffix[c, r, 0] = jnp.zeros((SUB, wide), jnp.bfloat16)
+        for r in range(HALF):
+            suffix[r, 0] = jnp.zeros((SUB, width), jnp.bfloat16)
 
     load_act.wait()
     total = None
-    for c in range(CHUNKS):
+    for c in range(2):
         load_enc[c].wait()
-        term = jnp.dot(
-            act[:, c * wide : (c + 1) * wide], enc[c * wide : (c + 1) * wide, :], preferred_element_type=jnp.float32
-        )
+        deep = slice(c * (width // 2), (c + 1) * (width // 2))
+        term = jnp.dot(act[:, deep], enc[deep, :], preferred_element_type=jnp.float32)
         total = term if total is None else total + term
     part[...] = total
     pl.semaphore_wait(barrier, HALF + 1)
@@ -169,6 +184,8 @@
     tokens = act.shape[0]
     below = (lax.broadcasted_iota(jnp.int32, (tokens, block), 1) + first) < cut
     load_mask.wait()
+    load_enc_bias.wait()
+    load_dec_bias.wait()
     kept = mask[...].astype(jnp.float32)
     load_dec.wait()
     swap.wait()
@@ -184,9 +201,9 @@
     def send_pieces(c, step, both):
         target = peer(step)
         if both:
-            src, dst = pieces_out.at[c, target], pieces.at[c, place]
+            src, dst = pieces_out.at[target, :, :, views[c]], pieces.at[place, :, :, views[c]]
         else:
-            src, dst = pieces_out.at[c, target, 1], pieces.at[c, place, 1]
+            src, dst = pieces_out.at[target, 1, :, views[c]], pieces.at[place, 1, :, views[c]]
         return remote(src, dst, a_send.at[c, step], a_recv.at[c, place], device(target))
 
     def wait_pieces(c, step):
@@ -194,20 +211,18 @@
 
         @pl.when(origin % 2 == 0)
         def _():
-            remote(
-                pieces_out.at[c, origin], pieces.at[c, origin], a_send.at[c, step], a_recv.at[c, origin], device(origin)
-            ).wait_recv()
+            ref = pieces.at[origin, :, :, views[c]]
+            remote(ref, ref, a_send.at[c, step], a_recv.at[c, origin], device(origin)).wait_recv()
 
         @pl.when(origin % 2 == 1)
         def _():
-            remote(
-                pieces_out.at[c, origin, 1], pieces.at[c, origin, 1], a_send.at[c, step], a_recv.at[c, origin],
-                device(origin),
-            ).wait_recv()
-
-    for c in range(CHUNKS):
-        made = jnp.dot(codes[...], dec[:, c * wide : (c + 1) * wide], preferred_element_type=jnp.float32)
-        pieces_out[c] = made.astype(jnp.bfloat16).reshape(HALF, 2, SUB, wide)
+            ref = pieces.at[origin, 1, :, views[c]]
+            remote(ref, ref, a_send.at[c, step], a_recv.at[c, origin], device(origin)).wait_recv()
+
+    for c in range(chunks):
+        span = spans[c]
+        made = jnp.dot(codes[...], dec[:, span], preferred_element_type=jnp.float32)
+        pieces_out[:, :, :, span] = made.astype(jnp.bfloat16).reshape(HALF, 2, SUB, span.stop - span.start)
 
         @pl.when(even)
         def _():
@@ -219,34 +234,34 @@
             for step in range(1, HALF):
                 send_pieces(c, step, False).start()
 
-        pieces[c, place] = pieces_out[c, place]
+        pieces[place, :, :, span] = pieces_out[place, :, :, span]
 
     crossing = []
-    for c in range(CHUNKS):
+    for c in range(chunks):
         for step in range(1, HALF):
             wait_pieces(c, step)
-        low0, seg = reduce_pieces(pieces, c)
+        low0, seg = reduce_pieces(pieces, spans[c])
         plain = ((low0 + seg[0]) + seg[1]) + (seg[2] + seg[3])
         weighted = ((5.0 * low0 + 4.0 * seg[0]) + 3.0 * seg[1]) + (2.0 * seg[2] + seg[3])
-        cross_out[c] = jnp.where(half == 0, plain, weighted).astype(jnp.bfloat16)
-        crossing.append(remote(cross_out.at[c], cross_in.at[c], x_send.at[c], x_recv.at[c], other_half))
+        cross_out[:, spans[c]] = jnp.where(half == 0, plain, weighted).astype(jnp.bfloat16)
+        crossing.append(remote(cross_out.at[:, views[c]], cross_in.at[:, views[c]], x_send.at[c], x_recv.at[c], other_half))
         crossing[-1].start()
 
     def send_suffix(c, step, both):
         target = peer(step)
         if both:
-            src, dst = tails.at[c, pl.ds(target // 2, 2)], suffix.at[c, place]
+            src, dst = tails.at[pl.ds(target // 2, 2), :, views[c]], suffix.at[place, :, :, views[c]]
         else:
-            src, dst = tails.at[c, target // 2 + 1], suffix.at[c, place, 1]
+            src, dst = tails.at[target // 2 + 1, :, views[c]], suffix.at[place, 1, :, views[c]]
         return remote(src, dst, b_send.at[c, step], b_recv.at[c, place], device(target))
 
     later = half.astype(jnp.float32)
     own_rows = pl.ds(pl.multiple_of(place * SUB, SUB), SUB)
-    for c in range(CHUNKS):
-        span = slice(c * wide, (c + 1) * wide)
-        low0, seg = reduce_pieces(pieces, c)
+    for c in range(chunks):
+        span = spans[c]
+        low0, seg = reduce_pieces(pieces, spans[c])
         crossing[c].wait_recv()
-        got = cross_in[c].astype(jnp.float32)
+        got = cross_in[:, span].astype(jnp.float32)
         base = dec_bias[:, span] - act[own_rows, span].astype(jnp.float32)
         before = base + later * (got + low0)
         errors = []
@@ -261,7 +276,7 @@
             scaled.append(tail)
         scaled.append(tail + before)
         for k in range(5):
-            tails[c, k] = (scaled[4 - k] / GROUPS).astype(jnp.bfloat16)
+            tails[k, :, span] = (scaled[4 - k] / GROUPS).astype(jnp.bfloat16)
         row_out[:, span] = jnp.sum(scaled[3] / GROUPS, axis=0, keepdims=True)
         for step in range(1, HALF):
 
@@ -273,7 +288,7 @@
             def _():
                 send_suffix(c, step, False).start()
 
-        suffix[c, place] = tails[c, pl.ds(place // 2, 2)]
+        suffix[place, :, :, span] = tails[pl.ds(place // 2, 2), :, span]
 
     def row_copy(step):
         return remote(row_out, rows.at[place], r_send.at[step], r_recv.at[place], device(peer(step)))
@@ -284,29 +299,28 @@
 
     back = None
     stores = []
-    for c in range(CHUNKS):
+    for c in range(chunks):
 
         @pl.when(even)
         def _():
             for step in range(1, HALF):
                 origin = source(step)
-                remote(
-                    suffix.at[c, origin], suffix.at[c, origin], b_send.at[c, step], b_recv.at[c, origin], device(origin)
-                ).wait_recv()
+                ref = suffix.at[origin, :, :, views[c]]
+                remote(ref, ref, b_send.at[c, step], b_recv.at[c, origin], device(origin)).wait_recv()
 
         @pl.when(odd)
         def _():
             for step in range(1, HALF):
                 origin = source(step)
-                remote(
-                    suffix.at[c, origin, 1], suffix.at[c, origin, 1], b_send.at[c, step], b_recv.at[c, origin],
-                    device(origin),
-                ).wait_recv()
-
-        stores.append(pltpu.make_async_copy(suffix.at[c], suffix_out.at[c], store_sems.at[1 + c]))
+                ref = suffix.at[origin, 1, :, views[c]]
+                remote(ref, ref, b_send.at[c, step], b_recv.at[c, origin], device(origin)).wait_recv()
+
+        span = spans[c]
+        there = suffix_out.at[:, :, :, views[c]]
+        stores.append(pltpu.make_async_copy(suffix.at[:, :, :, views[c]], there, store_sems.at[1 + c]))
         stores[-1].start()
         term = lax.dot_general(
-            suffix[c].reshape(2 * tokens, wide), dec[:, c * wide : (c + 1) * wide],
+            suffix[:, :, :, span].reshape(2 * tokens, span.stop - span.start), dec[:, span],
             (((1,), (1,)), ((), ())), preferred_element_type=jnp.float32,
         )
         back = term if back is None else back + term
@@ -323,7 +337,7 @@
     for r in range(1, HALF):
         summed = summed + rows[r]
     final_out[...] = summed
-    finish = remote(final_out, final_in, x_send.at[CHUNKS], x_recv.at[CHUNKS], other_half)
+    finish = remote(final_out, final_in, x_send.at[chunks], x_recv.at[chunks], other_half)
     finish.start()
 
     swap_back.wait()
@@ -331,7 +345,7 @@
     enc_bias_out[...] = jnp.sum(pre, axis=0, keepdims=True)
     pre_out[...] = pre.astype(jnp.bfloat16)
 
-    for c in range(CHUNKS):
+    for c in range(chunks):
         crossing[c].wait_send()
 
         @pl.when(even)
@@ -369,18 +383,19 @@
         jnp.bfloat16
     )
     dec_grad[...] = lax.dot_general(
-        codes[...], suffix[0], contract_rows, preferred_element_type=jnp.float32
+        codes[...], suffix[...], contract_rows, preferred_element_type=jnp.float32
     ).astype(jnp.bfloat16)
-    enc_bias_out[...] = enc_bias_in[...]
-    dec_bias_out[...] = dec_bias_in[...]
+    enc_bias_out[...] = enc_bias_in[0]
+    dec_bias_out[...] = dec_bias_in[0]
 
 
 def kernel_body(activations, encoder, encoder_bias, decoder, decoder_bias, kept_mask, boundaries):
     tokens, width = activations.shape
     block = encoder.shape[1]
-    wide = width // CHUNKS
+    chunks = len(column_chunks(width))
+    wide = width // STEPS
     low, full = jnp.bfloat16, jnp.float32
-    hbm = pl.BlockSpec(memory_space=pl.ANY)
+    hbm = pl.BlockSpec(memory_space=pltpu.HBM)
     vmem = pl.BlockSpec(memory_space=pltpu.VMEM)
     smem = pl.BlockSpec(memory_space=pltpu.SMEM)
     dma = pltpu.SemaphoreType.DMA
@@ -388,81 +403,82 @@
         exchange_kernel,
         out_shape=[
             jax.ShapeDtypeStruct((2 * tokens, block), low),
-            jax.ShapeDtypeStruct((CHUNKS, HALF, 2, SUB, wide), low),
+            jax.ShapeDtypeStruct((HALF, 2, SUB, width), low),
             jax.ShapeDtypeStruct((tokens, block), low),
             jax.ShapeDtypeStruct((1, block), full),
             jax.ShapeDtypeStruct((1, width), full),
         ],
-        in_specs=[hbm, hbm, vmem, hbm, vmem, hbm, smem],
+        in_specs=[hbm, hbm, hbm, hbm, hbm, hbm, smem],
         out_specs=[hbm, hbm, vmem, vmem, vmem],
         scratch_shapes=[
             pltpu.VMEM((tokens, width), low),
             pltpu.VMEM((width, block), low),
+            pltpu.VMEM((1, block), full),
             pltpu.VMEM((block, width), low),
+            pltpu.VMEM((1, width), full),
             pltpu.VMEM((tokens, block), jnp.int32),
             pltpu.VMEM((tokens, block), full),
             pltpu.VMEM((tokens, block), full),
             pltpu.VMEM((tokens, block), full),
             pltpu.VMEM((tokens, block), full),
             pltpu.VMEM((2 * tokens, block), low),
-            pltpu.VMEM((CHUNKS, HALF, 2, SUB, wide), low),
-            pltpu.VMEM((CHUNKS, HALF, 2, SUB, wide), low),
-            pltpu.VMEM((CHUNKS, SUB, wide), low),
-            pltpu.VMEM((CHUNKS, SUB, wide), low),
-            pltpu.VMEM((CHUNKS, 5, SUB, wide), low),
-            pltpu.VMEM((CHUNKS, HALF, 2, SUB, wide), low),
+            pltpu.VMEM((HALF, 2, SUB, width), low),
+            pltpu.VMEM((HALF, 2, SUB, width), low),
+            pltpu.VMEM((SUB, width), low),
+            pltpu.VMEM((SUB, width), low),
+            pltpu.VMEM((5, SUB, width), low),
+            pltpu.VMEM((HALF, 2, SUB, width), low),
             pltpu.VMEM((1, width), full),
             pltpu.VMEM((HALF, 1, width), full),
             pltpu.VMEM((1, width), full),
             pltpu.VMEM((1, width), full),
-            dma((3 + CHUNKS,)),
+            dma((7,)),
             dma((4,)),
-            dma((CHUNKS, HALF)),
-            dma((CHUNKS, HALF)),
-            dma((CHUNKS + 1,)),
-            dma((CHUNKS + 1,)),
-            dma((CHUNKS, HALF)),
-            dma((CHUNKS, HALF)),
+            dma((chunks, HALF)),
+            dma((chunks, HALF)),
+            dma((chunks + 1,)),
+            dma((chunks + 1,)),
+            dma((chunks, HALF)),
+            dma((chunks, HALF)),
             dma((HALF,)),
             dma((HALF,)),
-            dma((1 + CHUNKS,)),
+            dma((1 + chunks,)),
         ],
         compiler_params=pltpu.CompilerParams(
-            collective_id=0, has_side_effects=True, vmem_limit_bytes=40 * 1024 * 1024
+            collective_id=0, has_side_effects=True, vmem_limit_bytes=60 * 1024 * 1024
         ),
         name="exchange",
     )(
-        activations, encoder, encoder_bias.reshape(1, block), decoder, decoder_bias.reshape(1, width), kept_mask,
-        boundaries,
-    )
-    suffix = suffix.reshape(CHUNKS, 2 * tokens, wide)
+        activations, encoder, encoder_bias, decoder, decoder_bias, kept_mask, boundaries,
+    )
+    suffix = suffix.reshape(2 * tokens, width)
     enc_grad, dec_grad, enc_bias_grad, dec_bias_grad = pl.pallas_call(
         grads_kernel,
-        grid=(CHUNKS,),
+        grid=(STEPS,),
         out_shape=[
             jax.ShapeDtypeStruct((width, block), low),
             jax.ShapeDtypeStruct((block, width), low),
-            jax.ShapeDtypeStruct((1, block), full),
-            jax.ShapeDtypeStruct((1, width), full),
+            jax.ShapeDtypeStruct((block,), full),
+            jax.ShapeDtypeStruct((width,), full),
         ],
         in_specs=[
             pl.BlockSpec((tokens, wide), lambda c: (0, c)),
             pl.BlockSpec((tokens, block), lambda c: (0, 0)),
             pl.BlockSpec((2 * tokens, block), lambda c: (0, 0)),
-            pl.BlockSpec((1, 2 * tokens, wide), lambda c: (c, 0, 0)),
+            pl.BlockSpec((2 * tokens, wide), lambda c: (0, c)),
             pl.BlockSpec((1, block), lambda c: (0, 0)),
             pl.BlockSpec((1, width), lambda c: (0, 0)),
         ],
         out_specs=[
             pl.BlockSpec((wide, block), lambda c: (c, 0)),
             pl.BlockSpec((block, wide), lambda c: (0, c)),
-            pl.BlockSpec((1, block), lambda c: (0, 0)),
-            pl.BlockSpec((1, width), lambda c: (0, 0)),
+            pl.BlockSpec((block,), lambda c: (0,)),
+            pl.BlockSpec((width,), lambda c: (0,)),
         ],
-        compiler_params=pltpu.CompilerParams(vmem_limit_bytes=32 * 1024 * 1024),
+        compiler_params=pltpu.CompilerParams(vmem_limit_bytes=60 * 1024 * 1024),
         name="grads",
     )(activations, pre, codes, suffix, enc_bias_grad, dec_bias_grad)
-    return enc_grad, enc_bias_grad.reshape(block), dec_grad, dec_bias_grad.reshape(width)
+    return enc_grad, enc_bias_grad, dec_grad, dec_bias_grad
 
 
 def fits(mesh):

time: 48.5 us -> 43.1 us (0.89)
  local copies, waits for them, and re-layouts: 7 us -> 0 us
  Pallas kernels: 39.9 us -> 42.3 us
  other arithmetic: 0.62 us -> 0 us
    unnamed x12 -> x0, local copies, waits for them, and re-layouts: 6.3 us -> none
    pallas_call x1, Pallas kernels: 2.44 us -> 3.68 us  [kernel_body(): pl.pallas_call(grads_kernel, grid=(STEPS,), out_shape=[jax.ShapeDtypeStru...]
    pallas_call x1, Pallas kernels: 37.4 us -> 38.6 us  [kernel_body(): pl.pallas_call(exchange_kernel, out_shape=[jax.ShapeDtypeStruct((2 * toke...]
    reshape x1 -> x0, local copies, waits for them, and re-layouts: 0.7 us -> none  [kernel_body(): decoder_bias.reshape(1, width)]
    pallas_call x1 -> x0, other arithmetic: 0.62 us -> none  [kernel_body(): pl.pallas_call(grads_kernel, grid=(CHUNKS,), out_shape=[jax.ShapeDtypeStr...]
where the time goes in v2:
time: 43.1 us; the launch traced here: 42.9 us
  Pallas kernels  42.3 us (98%)
  between operations  0.64 us (1%)
    pallas_call x1, Pallas kernels, kernel_body(): pl.pallas_call(exchange_kernel, out_shape=[jax.ShapeDtypeStruct((2 * toke...  38.6 us
    pallas_call x1, Pallas kernels, kernel_body(): pl.pallas_call(grads_kernel, grid=(STEPS,), out_shape=[jax.ShapeDtypeStru...  3.68 us

profile of v2, /device:TPU:0, one launch (start us, length us, event | category | flops | bytes accessed | tf_op | source)
XLA Modules:
  0.0 42.9 jit_solution(5036655666206911179)
XLA Ops:
  0.6 38.6 %exchange.1 = (bf16[256,512]{1,0:T(8,128)(2,1)}, bf16[8,2,16,1792]{3,2,1,0:T(8,128)(2,1)}, bf16[128,512]{1,0:T(8,128)(2,1)}, f32[1,512]{1,0:T(1,128)}, f32[1,1792]{1,0:T(1,128)}) custom-call(bf16[128,1792]{1,0:T(8,128)(2,1)} %act.1, bf16[1792,512]{1,0:T(8,128)(2,1)} %enc_hbm.1, f32[512]{0:T(512)} %enc_bias_hbm.1, bf16[512,1792]{1,0:T(8,128)(2,1)} %dec_hbm.1, ...), custom_call_target="tpu_custom_call" | custom-call | tf_op jit(solution)/shard_map/exchange/pallas_call | solution.py:402
  39.2 3.7 %grads.1 = (bf16[1792,512]{1,0:T(8,128)(2,1)}, bf16[512,1792]{1,0:T(8,128)(2,1)}, f32[512]{0:T(512)}, f32[1792]{0:T(1024)}) custom-call(bf16[128,1792]{1,0:T(8,128)(2,1)} %act.1, bf16[128,512]{1,0:T(8,128)(2,1)} %get-tuple-element.13.pre, bf16[256,512]{1,0:T(8,128)(2,1)} %get-tuple-element.14.codes, bf16[256,1792]{1,0:T(8,128)(2,1)} %bitcast.1, ...), custom_call_target="tpu_custom_call" | custom-call | tf_op jit(solution)/shard_map/grads/pallas_call | solution.py:455

commit v3 on v2

--- a/solution.py
+++ b/solution.py
@@ -11,7 +11,7 @@
 HALF = 8
 SUB = 16
 LANES = 128
-STEPS = 2
+STEPS = 7
 MESH = pl.DeviceIdType.MESH
 
 
@@ -85,7 +85,7 @@
     tiles = width // LANES
     widths = []
     while tiles > 0:
-        widths.append(min(2 if not widths else 4, tiles))
+        widths.append(min(4 if len(widths) in (1, 2) else 2, tiles))
         tiles -= widths[-1]
     ends = [LANES * sum(widths[: k + 1]) for k in range(len(widths))]
     return [slice(end - LANES * count, end) for end, count in zip(ends, widths)]
@@ -237,14 +237,17 @@
         pieces[place, :, :, span] = pieces_out[place, :, :, span]
 
     crossing = []
-    for c in range(chunks):
+
+    def cross(c):
         for step in range(1, HALF):
             wait_pieces(c, step)
         low0, seg = reduce_pieces(pieces, spans[c])
         plain = ((low0 + seg[0]) + seg[1]) + (seg[2] + seg[3])
         weighted = ((5.0 * low0 + 4.0 * seg[0]) + 3.0 * seg[1]) + (2.0 * seg[2] + seg[3])
         cross_out[:, spans[c]] = jnp.where(half == 0, plain, weighted).astype(jnp.bfloat16)
-        crossing.append(remote(cross_out.at[:, views[c]], cross_in.at[:, views[c]], x_send.at[c], x_recv.at[c], other_half))
+        crossing.append(
+            remote(cross_out.at[:, views[c]], cross_in.at[:, views[c]], x_send.at[c], x_recv.at[c], other_half)
+        )
         crossing[-1].start()
 
     def send_suffix(c, step, both):
@@ -257,7 +260,7 @@
 
     later = half.astype(jnp.float32)
     own_rows = pl.ds(pl.multiple_of(place * SUB, SUB), SUB)
-    for c in range(chunks):
+    def finalize(c):
         span = spans[c]
         low0, seg = reduce_pieces(pieces, spans[c])
         crossing[c].wait_recv()
@@ -289,6 +292,12 @@
                 send_suffix(c, step, False).start()
 
         suffix[place, :, :, span] = tails[pl.ds(place // 2, 2), :, span]
+
+    for c in range(chunks + 1):
+        if c < chunks:
+            cross(c)
+        if c > 0:
+            finalize(c - 1)
 
     def row_copy(step):
         return remote(row_out, rows.at[place], r_send.at[step], r_recv.at[place], device(peer(step)))

time: 43.1 us -> 44 us (1.021)
  Pallas kernels: 42.3 us -> 43.1 us
    pallas_call x1, Pallas kernels: 3.68 us -> 6.42 us  [kernel_body(): pl.pallas_call(grads_kernel, grid=(STEPS,), out_shape=[jax.ShapeDtypeStru...]
    pallas_call x1, Pallas kernels: 38.6 us -> 36.7 us  [kernel_body(): pl.pallas_call(exchange_kernel, out_shape=[jax.ShapeDtypeStruct((2 * toke...]
where the time goes in v3:
time: 44 us; the launch traced here: 43.8 us
  Pallas kernels  43.1 us (98%)
  between operations  0.64 us (1%)
    pallas_call x1, Pallas kernels, kernel_body(): pl.pallas_call(exchange_kernel, out_shape=[jax.ShapeDtypeStruct((2 * toke...  36.7 us
    pallas_call x1, Pallas kernels, kernel_body(): pl.pallas_call(grads_kernel, grid=(STEPS,), out_shape=[jax.ShapeDtypeStru...  6.42 us

profile of v3, /device:TPU:0, one launch (start us, length us, event | category | flops | bytes accessed | tf_op | source)
XLA Modules:
  0.0 43.8 jit_solution(4818132105478017147)
XLA Ops:
  0.6 36.7 %exchange.1 = (bf16[256,512]{1,0:T(8,128)(2,1)}, bf16[8,2,16,1792]{3,2,1,0:T(8,128)(2,1)}, bf16[128,512]{1,0:T(8,128)(2,1)}, f32[1,512]{1,0:T(1,128)}, f32[1,1792]{1,0:T(1,128)}) custom-call(bf16[128,1792]{1,0:T(8,128)(2,1)} %act.1, bf16[1792,512]{1,0:T(8,128)(2,1)} %enc_hbm.1, f32[512]{0:T(512)} %enc_bias_hbm.1, bf16[512,1792]{1,0:T(8,128)(2,1)} %dec_hbm.1, ...), custom_call_target="tpu_custom_call" | custom-call | tf_op jit(solution)/shard_map/exchange/pallas_call | solution.py:411
  37.3 6.4 %grads.1 = (bf16[1792,512]{1,0:T(8,128)(2,1)}, bf16[512,1792]{1,0:T(8,128)(2,1)}, f32[512]{0:T(512)}, f32[1792]{0:T(1024)}) custom-call(bf16[128,1792]{1,0:T(8,128)(2,1)} %act.1, bf16[128,512]{1,0:T(8,128)(2,1)} %get-tuple-element.13.pre, bf16[256,512]{1,0:T(8,128)(2,1)} %get-tuple-element.14.codes, bf16[256,1792]{1,0:T(8,128)(2,1)} %bitcast.1, ...), custom_call_target="tpu_custom_call" | custom-call | tf_op jit(solution)/shard_map/grads/pallas_call | solution.py:464

commit v4 on v3

--- a/solution.py
+++ b/solution.py
@@ -11,7 +11,8 @@
 HALF = 8
 SUB = 16
 LANES = 128
-STEPS = 7
+AHEAD = 3
+PARTS = 2
 MESH = pl.DeviceIdType.MESH
 
 
@@ -85,7 +86,7 @@
     tiles = width // LANES
     widths = []
     while tiles > 0:
-        widths.append(min(4 if len(widths) in (1, 2) else 2, tiles))
+        widths.append(min(2, tiles))
         tiles -= widths[-1]
     ends = [LANES * sum(widths[: k + 1]) for k in range(len(widths))]
     return [slice(end - LANES * count, end) for end, count in zip(ends, widths)]
@@ -106,7 +107,7 @@
     codes_out, suffix_out, pre_out, enc_bias_out, dec_bias_out,
     act, enc, enc_bias, dec, dec_bias, mask, part, part_in, grad, grad_in, codes,
     pieces_out, pieces, cross_out, cross_in, tails, suffix,
-    row_out, rows, final_out, final_in,
+    row_out, rows, final_out, final_in, pre_low, enc_bias_row, dec_bias_row,
     load_sems, wid_sems, a_send, a_recv, x_send, x_recv, b_send, b_recv, r_send, r_recv, store_sems,
 ):
     lat = lax.axis_index("lat")
@@ -219,7 +220,7 @@
             ref = pieces.at[origin, 1, :, views[c]]
             remote(ref, ref, a_send.at[c, step], a_recv.at[c, origin], device(origin)).wait_recv()
 
-    for c in range(chunks):
+    def make(c):
         span = spans[c]
         made = jnp.dot(codes[...], dec[:, span], preferred_element_type=jnp.float32)
         pieces_out[:, :, :, span] = made.astype(jnp.bfloat16).reshape(HALF, 2, SUB, span.stop - span.start)
@@ -260,6 +261,7 @@
 
     later = half.astype(jnp.float32)
     own_rows = pl.ds(pl.multiple_of(place * SUB, SUB), SUB)
+
     def finalize(c):
         span = spans[c]
         low0, seg = reduce_pieces(pieces, spans[c])
@@ -293,9 +295,13 @@
 
         suffix[place, :, :, span] = tails[pl.ds(place // 2, 2), :, span]
 
+    for c in range(min(AHEAD, chunks)):
+        make(c)
     for c in range(chunks + 1):
         if c < chunks:
             cross(c)
+        if c + AHEAD < chunks:
+            make(c + AHEAD)
         if c > 0:
             finalize(c - 1)
 
@@ -351,8 +357,12 @@
 
     swap_back.wait()
     pre = kept * (grad[...] + grad_in[...])
-    enc_bias_out[...] = jnp.sum(pre, axis=0, keepdims=True)
-    pre_out[...] = pre.astype(jnp.bfloat16)
+    pre_low[...] = pre.astype(jnp.bfloat16)
+    stores.append(pltpu.make_async_copy(pre_low, pre_out, store_sems.at[1 + chunks]))
+    stores[-1].start()
+    enc_bias_row[...] = jnp.sum(pre, axis=0, keepdims=True)
+    stores.append(pltpu.make_async_copy(enc_bias_row, enc_bias_out, store_sems.at[2 + chunks]))
+    stores[-1].start()
 
     for c in range(chunks):
         crossing[c].wait_send()
@@ -380,32 +390,63 @@
     for step in range(1, HALF):
         row_copy(step).wait_send()
     finish.wait()
-    dec_bias_out[...] = jnp.where(half == 0, final_out[...], final_in[...])
+    dec_bias_row[...] = jnp.where(half == 0, final_out[...], final_in[...])
+    stores.append(pltpu.make_async_copy(dec_bias_row, dec_bias_out, store_sems.at[3 + chunks]))
+    stores[-1].start()
     store_codes.wait()
     for store in stores:
         store.wait()
 
 
-def grads_kernel(act, pre, codes, suffix, enc_bias_in, dec_bias_in, enc_grad, dec_grad, enc_bias_out, dec_bias_out):
+def grads_kernel(
+    act_hbm, pre_hbm, codes_hbm, suffix_hbm, enc_bias_in, dec_bias_in,
+    enc_out, dec_out, enc_bias_out, dec_bias_out,
+    act, pre, codes, suffix, enc_grad, dec_grad, load_sems, store_sems,
+):
     contract_rows = (((0,), (0,)), ((), ()))
-    enc_grad[...] = lax.dot_general(act[...], pre[...], contract_rows, preferred_element_type=jnp.float32).astype(
-        jnp.bfloat16
-    )
-    dec_grad[...] = lax.dot_general(
-        codes[...], suffix[...], contract_rows, preferred_element_type=jnp.float32
-    ).astype(jnp.bfloat16)
-    enc_bias_out[...] = enc_bias_in[0]
-    dec_bias_out[...] = dec_bias_in[0]
+    width = act.shape[1]
+    part = width // PARTS
+    pairs = ((pre_hbm, pre), (act_hbm, act), (codes_hbm, codes), (suffix_hbm, suffix))
+    loads = [pltpu.make_async_copy(src, dst, load_sems.at[k]) for k, (src, dst) in enumerate(pairs)]
+    for load in loads:
+        load.start()
+    stores = [
+        pltpu.make_async_copy(enc_bias_in.at[0], enc_bias_out, store_sems.at[0]),
+        pltpu.make_async_copy(dec_bias_in.at[0], dec_bias_out, store_sems.at[1]),
+    ]
+    for store in stores:
+        store.start()
+
+    def put(src, dst):
+        stores.append(pltpu.make_async_copy(src, dst, store_sems.at[len(stores)]))
+        stores[-1].start()
+
+    loads[0].wait()
+    loads[1].wait()
+    for k in range(PARTS):
+        span, view = slice(k * part, (k + 1) * part), pl.ds(k * part, part)
+        enc_grad[span, :] = lax.dot_general(
+            act[:, span], pre[...], contract_rows, preferred_element_type=jnp.float32
+        ).astype(jnp.bfloat16)
+        put(enc_grad.at[view, :], enc_out.at[view, :])
+    loads[2].wait()
+    loads[3].wait()
+    for k in range(PARTS):
+        span, view = slice(k * part, (k + 1) * part), pl.ds(k * part, part)
+        dec_grad[:, span] = lax.dot_general(
+            codes[...], suffix[:, span], contract_rows, preferred_element_type=jnp.float32
+        ).astype(jnp.bfloat16)
+        put(dec_grad.at[:, view], dec_out.at[:, view])
+    for store in stores:
+        store.wait()
 
 
 def kernel_body(activations, encoder, encoder_bias, decoder, decoder_bias, kept_mask, boundaries):
     tokens, width = activations.shape
     block = encoder.shape[1]
     chunks = len(column_chunks(width))
-    wide = width // STEPS
     low, full = jnp.bfloat16, jnp.float32
     hbm = pl.BlockSpec(memory_space=pltpu.HBM)
-    vmem = pl.BlockSpec(memory_space=pltpu.VMEM)
     smem = pl.BlockSpec(memory_space=pltpu.SMEM)
     dma = pltpu.SemaphoreType.DMA
     codes, suffix, pre, enc_bias_grad, dec_bias_grad = pl.pallas_call(
@@ -418,7 +459,7 @@
             jax.ShapeDtypeStruct((1, width), full),
         ],
         in_specs=[hbm, hbm, hbm, hbm, hbm, hbm, smem],
-        out_specs=[hbm, hbm, vmem, vmem, vmem],
+        out_specs=[hbm, hbm, hbm, hbm, hbm],
         scratch_shapes=[
             pltpu.VMEM((tokens, width), low),
             pltpu.VMEM((width, block), low),
@@ -441,6 +482,9 @@
             pltpu.VMEM((HALF, 1, width), full),
             pltpu.VMEM((1, width), full),
             pltpu.VMEM((1, width), full),
+            pltpu.VMEM((tokens, block), low),
+            pltpu.VMEM((1, block), full),
+            pltpu.VMEM((1, width), full),
             dma((7,)),
             dma((4,)),
             dma((chunks, HALF)),
@@ -451,7 +495,7 @@
             dma((chunks, HALF)),
             dma((HALF,)),
             dma((HALF,)),
-            dma((1 + chunks,)),
+            dma((4 + chunks,)),
         ],
         compiler_params=pltpu.CompilerParams(
             collective_id=0, has_side_effects=True, vmem_limit_bytes=60 * 1024 * 1024
@@ -463,26 +507,23 @@
     suffix = suffix.reshape(2 * tokens, width)
     enc_grad, dec_grad, enc_bias_grad, dec_bias_grad = pl.pallas_call(
         grads_kernel,
-        grid=(STEPS,),
         out_shape=[
             jax.ShapeDtypeStruct((width, block), low),
             jax.ShapeDtypeStruct((block, width), low),
             jax.ShapeDtypeStruct((block,), full),
             jax.ShapeDtypeStruct((width,), full),
         ],
-        in_specs=[
-            pl.BlockSpec((tokens, wide), lambda c: (0, c)),
-            pl.BlockSpec((tokens, block), lambda c: (0, 0)),
-            pl.BlockSpec((2 * tokens, block), lambda c: (0, 0)),
-            pl.BlockSpec((2 * tokens, wide), lambda c: (0, c)),
-            pl.BlockSpec((1, block), lambda c: (0, 0)),
-            pl.BlockSpec((1, width), lambda c: (0, 0)),
-        ],
-        out_specs=[
-            pl.BlockSpec((wide, block), lambda c: (c, 0)),
-            pl.BlockSpec((block, wide), lambda c: (0, c)),
-            pl.BlockSpec((block,), lambda c: (0,)),
-            pl.BlockSpec((width,), lambda c: (0,)),
+        in_specs=[hbm] * 6,
+        out_specs=[hbm] * 4,
+        scratch_shapes=[
+            pltpu.VMEM((tokens, width), low),
+            pltpu.VMEM((tokens, block), low),
+            pltpu.VMEM((2 * tokens, block), low),
+            pltpu.VMEM((2 * tokens, width), low),
+            pltpu.VMEM((width, block), low),
+            pltpu.VMEM((block, width), low),
+            dma((4,)),
+            dma((2 + 2 * PARTS,)),
         ],
         compiler_params=pltpu.CompilerParams(vmem_limit_bytes=60 * 1024 * 1024),
         name="grads",

time: 44 us -> 42.6 us (0.968)
  Pallas kernels: 43.1 us -> 41.8 us
    pallas_call x1, Pallas kernels: 6.42 us -> 3.53 us  [kernel_body(): pl.pallas_call(grads_kernel, out_shape=[jax.ShapeDtypeStruct((width, bloc...]
    pallas_call x1, Pallas kernels: 36.7 us -> 38.3 us  [kernel_body(): pl.pallas_call(exchange_kernel, out_shape=[jax.ShapeDtypeStruct((2 * toke...]
where the time goes in v4:
time: 42.6 us; the launch traced here: 42.4 us
  Pallas kernels  41.8 us (98%)
  between operations  0.64 us (2%)
    pallas_call x1, Pallas kernels, kernel_body(): pl.pallas_call(exchange_kernel, out_shape=[jax.ShapeDtypeStruct((2 * toke...  38.3 us
    pallas_call x1, Pallas kernels, kernel_body(): pl.pallas_call(grads_kernel, out_shape=[jax.ShapeDtypeStruct((width, bloc...  3.53 us

profile of v4, /device:TPU:0, one launch (start us, length us, event | category | flops | bytes accessed | tf_op | source)
XLA Modules:
  0.0 42.4 jit_solution(13545745333287763640)
XLA Ops:
  0.6 38.3 %exchange.1 = (bf16[256,512]{1,0:T(8,128)(2,1)}, bf16[8,2,16,1792]{3,2,1,0:T(8,128)(2,1)}, bf16[128,512]{1,0:T(8,128)(2,1)}, f32[1,512]{1,0:T(1,128)}, f32[1,1792]{1,0:T(1,128)}) custom-call(bf16[128,1792]{1,0:T(8,128)(2,1)} %act_hbm.3, bf16[1792,512]{1,0:T(8,128)(2,1)} %enc_hbm.1, f32[512]{0:T(512)} %enc_bias_hbm.1, bf16[512,1792]{1,0:T(8,128)(2,1)} %dec_hbm.1, ...), custom_call_target="tpu_custom_call" | custom-call | tf_op jit(solution)/shard_map/exchange/pallas_call | solution.py:452
  38.9 3.5 %grads.1 = (bf16[1792,512]{1,0:T(8,128)(2,1)}, bf16[512,1792]{1,0:T(8,128)(2,1)}, f32[512]{0:T(512)}, f32[1792]{0:T(1024)}) custom-call(bf16[128,1792]{1,0:T(8,128)(2,1)} %act_hbm.3, bf16[128,512]{1,0:T(8,128)(2,1)} %get-tuple-element.13.pre_hbm, bf16[256,512]{1,0:T(8,128)(2,1)} %get-tuple-element.14.codes_hbm, bf16[256,1792]{1,0:T(8,128)(2,1)} %bitcast.1, ...), custom_call_target="tpu_custom_call" | custom-call | tf_op jit(solution)/shard_map/grads/pallas_call | solution.py:508

commit v5 on v4

--- a/solution.py
+++ b/solution.py
@@ -11,7 +11,6 @@
 HALF = 8
 SUB = 16
 LANES = 128
-AHEAD = 3
 PARTS = 2
 MESH = pl.DeviceIdType.MESH
 
@@ -86,7 +85,7 @@
     tiles = width // LANES
     widths = []
     while tiles > 0:
-        widths.append(min(2, tiles))
+        widths.append(min(4 if len(widths) in (1, 2) else 2, tiles))
         tiles -= widths[-1]
     ends = [LANES * sum(widths[: k + 1]) for k in range(len(widths))]
     return [slice(end - LANES * count, end) for end, count in zip(ends, widths)]
@@ -104,10 +103,11 @@
 
 def exchange_kernel(
     act_hbm, enc_hbm, enc_bias_hbm, dec_hbm, dec_bias_hbm, mask_hbm, bounds,
-    codes_out, suffix_out, pre_out, enc_bias_out, dec_bias_out,
+    act_out, dec_grad_out, pre_out, enc_bias_out, dec_bias_out,
     act, enc, enc_bias, dec, dec_bias, mask, part, part_in, grad, grad_in, codes,
     pieces_out, pieces, cross_out, cross_in, tails, suffix,
     row_out, rows, final_out, final_in, pre_low, enc_bias_row, dec_bias_row,
+    act_turned, codes_turned, dec_grad,
     load_sems, wid_sems, a_send, a_recv, x_send, x_recv, b_send, b_recv, r_send, r_recv, store_sems,
 ):
     lat = lax.axis_index("lat")
@@ -121,6 +121,8 @@
     chunks = len(spans)
     views = [pl.ds(span.start, span.stop - span.start) for span in spans]
     block = dec.shape[0]
+    halves = [slice(0, block // 2), slice(block // 2, block)]
+    sides = [pl.ds(0, block // 2), pl.ds(block // 2, block // 2)]
     other_core = {"lat": lat, "wid": 1 - wid}
     other_half = {"lat": (lat + HALF) % (2 * HALF), "wid": wid}
 
@@ -148,8 +150,7 @@
     load_act.start()
     load_enc = []
     for c in range(2):
-        rows_of = pl.ds(c * (width // 2), width // 2)
-        load_enc.append(pltpu.make_async_copy(enc_hbm.at[rows_of], enc.at[rows_of], load_sems.at[1 + c]))
+        load_enc.append(pltpu.make_async_copy(enc_hbm.at[:, sides[c]], enc.at[:, sides[c]], load_sems.at[1 + c]))
         load_enc[-1].start()
     load_mask = pltpu.make_async_copy(mask_hbm, mask, load_sems.at[3])
     load_mask.start()
@@ -166,16 +167,15 @@
             suffix[r, 0] = jnp.zeros((SUB, width), jnp.bfloat16)
 
     load_act.wait()
-    total = None
+    swaps = []
     for c in range(2):
         load_enc[c].wait()
-        deep = slice(c * (width // 2), (c + 1) * (width // 2))
-        term = jnp.dot(act[:, deep], enc[deep, :], preferred_element_type=jnp.float32)
-        total = term if total is None else total + term
-    part[...] = total
-    pl.semaphore_wait(barrier, HALF + 1)
-    swap = remote(part, part_in, wid_sems.at[0], wid_sems.at[1], other_core)
-    swap.start()
+        part[:, halves[c]] = jnp.dot(act[...], enc[:, halves[c]], preferred_element_type=jnp.float32)
+        if c == 0:
+            pl.semaphore_wait(barrier, HALF + 1)
+        here, there = part.at[:, sides[c]], part_in.at[:, sides[c]]
+        swaps.append(remote(here, there, wid_sems.at[2 * c], wid_sems.at[2 * c + 1], other_core))
+        swaps[-1].start()
 
     first = lat * block
     cut = jnp.int32(0)
@@ -189,15 +189,14 @@
     load_dec_bias.wait()
     kept = mask[...].astype(jnp.float32)
     load_dec.wait()
-    swap.wait()
+    for swap in swaps:
+        swap.wait()
     full = kept * ((part[...] + part_in[...]) + enc_bias[...])
     low = jnp.where(below, full, 0.0).astype(jnp.bfloat16)
     high = jnp.where(below, 0.0, full).astype(jnp.bfloat16)
     for r in range(HALF):
         codes[2 * SUB * r : 2 * SUB * r + SUB, :] = low[SUB * r : SUB * (r + 1), :]
         codes[2 * SUB * r + SUB : 2 * SUB * (r + 1), :] = high[SUB * r : SUB * (r + 1), :]
-    store_codes = pltpu.make_async_copy(codes, codes_out, store_sems.at[0])
-    store_codes.start()
 
     def send_pieces(c, step, both):
         target = peer(step)
@@ -295,13 +294,15 @@
 
         suffix[place, :, :, span] = tails[pl.ds(place // 2, 2), :, span]
 
-    for c in range(min(AHEAD, chunks)):
+    for c in range(chunks):
         make(c)
+    act_turned[...] = act[...].T
+    stores = [pltpu.make_async_copy(act_turned, act_out, store_sems.at[1])]
+    stores[0].start()
+    codes_turned[...] = codes[...].T
     for c in range(chunks + 1):
         if c < chunks:
             cross(c)
-        if c + AHEAD < chunks:
-            make(c + AHEAD)
         if c > 0:
             finalize(c - 1)
 
@@ -312,8 +313,17 @@
         row_copy(step).start()
     rows[place] = row_out[...]
 
-    back = None
-    stores = []
+    below_parts = below.astype(jnp.float32).reshape(HALF, SUB, block) > 0.5
+    back = [None, None]
+    swaps_back = []
+
+    def grad_columns(c):
+        span = spans[c]
+        both = suffix[:, :, :, span].reshape(2 * tokens, span.stop - span.start)
+        dec_grad[:, span] = jnp.dot(codes_turned[...], both, preferred_element_type=jnp.float32).astype(jnp.bfloat16)
+        stores.append(pltpu.make_async_copy(dec_grad.at[:, views[c]], dec_grad_out.at[:, views[c]], store_sems.at[5 + c]))
+        stores[-1].start()
+
     for c in range(chunks):
 
         @pl.when(even)
@@ -331,19 +341,26 @@
                 remote(ref, ref, b_send.at[c, step], b_recv.at[c, origin], device(origin)).wait_recv()
 
         span = spans[c]
-        there = suffix_out.at[:, :, :, views[c]]
-        stores.append(pltpu.make_async_copy(suffix.at[:, :, :, views[c]], there, store_sems.at[1 + c]))
-        stores[-1].start()
-        term = lax.dot_general(
-            suffix[:, :, :, span].reshape(2 * tokens, span.stop - span.start), dec[:, span],
-            (((1,), (1,)), ((), ())), preferred_element_type=jnp.float32,
-        )
-        back = term if back is None else back + term
-    pair = back.reshape(HALF, 2, SUB, block)
-    below_parts = below.astype(jnp.float32).reshape(HALF, SUB, block) > 0.5
-    grad[...] = jnp.where(below_parts, pair[:, 0], pair[:, 1]).reshape(tokens, block)
-    swap_back = remote(grad, grad_in, wid_sems.at[2], wid_sems.at[3], other_core)
-    swap_back.start()
+        both = suffix[:, :, :, span].reshape(2 * tokens, span.stop - span.start)
+        for side in range(2):
+            term = lax.dot_general(
+                both, dec[halves[side], span], (((1,), (1,)), ((), ())), preferred_element_type=jnp.float32
+            )
+            back[side] = term if back[side] is None else back[side] + term
+            if c == chunks - 1:
+                pair = back[side].reshape(HALF, 2, SUB, block // 2)
+                chosen = jnp.where(below_parts[:, :, halves[side]], pair[:, 0], pair[:, 1])
+                grad[:, halves[side]] = chosen.reshape(tokens, block // 2)
+                here, there = grad.at[:, sides[side]], grad_in.at[:, sides[side]]
+                swaps_back.append(
+                    remote(here, there, wid_sems.at[4 + 2 * side], wid_sems.at[5 + 2 * side], other_core)
+                )
+                swaps_back[-1].start()
+        if c < chunks - 2:
+            grad_columns(c)
+
+    for c in range(chunks - 2, chunks):
+        grad_columns(c)
 
     for step in range(1, HALF):
         origin = source(step)
@@ -355,13 +372,14 @@
     finish = remote(final_out, final_in, x_send.at[chunks], x_recv.at[chunks], other_half)
     finish.start()
 
-    swap_back.wait()
+    for swap in swaps_back:
+        swap.wait()
     pre = kept * (grad[...] + grad_in[...])
     pre_low[...] = pre.astype(jnp.bfloat16)
-    stores.append(pltpu.make_async_copy(pre_low, pre_out, store_sems.at[1 + chunks]))
+    stores.append(pltpu.make_async_copy(pre_low, pre_out, store_sems.at[2]))
     stores[-1].start()
     enc_bias_row[...] = jnp.sum(pre, axis=0, keepdims=True)
-    stores.append(pltpu.make_async_copy(enc_bias_row, enc_bias_out, store_sems.at[2 + chunks]))
+    stores.append(pltpu.make_async_copy(enc_bias_row, enc_bias_out, store_sems.at[3]))
     stores[-1].start()
 
     for c in range(chunks):
@@ -391,52 +409,36 @@
         row_copy(step).wait_send()
     finish.wait()
     dec_bias_row[...] = jnp.where(half == 0, final_out[...], final_in[...])
-    stores.append(pltpu.make_async_copy(dec_bias_row, dec_bias_out, store_sems.at[3 + chunks]))
+    stores.append(pltpu.make_async_copy(dec_bias_row, dec_bias_out, store_sems.at[4]))
     stores[-1].start()
-    store_codes.wait()
     for store in stores:
         store.wait()
 
 
 def grads_kernel(
-    act_hbm, pre_hbm, codes_hbm, suffix_hbm, enc_bias_in, dec_bias_in,
+    act_hbm, pre_hbm, dec_grad_in, enc_bias_in, dec_bias_in,
     enc_out, dec_out, enc_bias_out, dec_bias_out,
-    act, pre, codes, suffix, enc_grad, dec_grad, load_sems, store_sems,
+    act, pre, enc_grad, load_sems, store_sems,
 ):
-    contract_rows = (((0,), (0,)), ((), ()))
-    width = act.shape[1]
-    part = width // PARTS
-    pairs = ((pre_hbm, pre), (act_hbm, act), (codes_hbm, codes), (suffix_hbm, suffix))
-    loads = [pltpu.make_async_copy(src, dst, load_sems.at[k]) for k, (src, dst) in enumerate(pairs)]
+    part = act.shape[0] // PARTS
+    loads = [
+        pltpu.make_async_copy(pre_hbm, pre, load_sems.at[0]),
+        pltpu.make_async_copy(act_hbm, act, load_sems.at[1]),
+    ]
+    stores = [
+        pltpu.make_async_copy(dec_grad_in, dec_out, store_sems.at[0]),
+        pltpu.make_async_copy(enc_bias_in.at[0], enc_bias_out, store_sems.at[1]),
+        pltpu.make_async_copy(dec_bias_in.at[0], dec_bias_out, store_sems.at[2]),
+    ]
+    for copy in loads + stores:
+        copy.start()
     for load in loads:
-        load.start()
-    stores = [
-        pltpu.make_async_copy(enc_bias_in.at[0], enc_bias_out, store_sems.at[0]),
-        pltpu.make_async_copy(dec_bias_in.at[0], dec_bias_out, store_sems.at[1]),
-    ]
-    for store in stores:
-        store.start()
-
-    def put(src, dst):
-        stores.append(pltpu.make_async_copy(src, dst, store_sems.at[len(stores)]))
-        stores[-1].start()
-
-    loads[0].wait()
-    loads[1].wait()
+        load.wait()
     for k in range(PARTS):
         span, view = slice(k * part, (k + 1) * part), pl.ds(k * part, part)
-        enc_grad[span, :] = lax.dot_general(
-            act[:, span], pre[...], contract_rows, preferred_element_type=jnp.float32
-        ).astype(jnp.bfloat16)
-        put(enc_grad.at[view, :], enc_out.at[view, :])
-    loads[2].wait()
-    loads[3].wait()
-    for k in range(PARTS):
-        span, view = slice(k * part, (k + 1) * part), pl.ds(k * part, part)
-        dec_grad[:, span] = lax.dot_general(
-            codes[...], suffix[:, span], contract_rows, preferred_element_type=jnp.float32
-        ).astype(jnp.bfloat16)
-        put(dec_grad.at[:, view], dec_out.at[:, view])
+        enc_grad[span, :] = jnp.dot(act[span, :], pre[...], preferred_element_type=jnp.float32).astype(jnp.bfloat16)
+        stores.append(pltpu.make_async_copy(enc_grad.at[view, :], enc_out.at[view, :], store_sems.at[3 + k]))
+        stores[-1].start()
     for store in stores:
         store.wait()
 
@@ -449,11 +451,11 @@
     hbm = pl.BlockSpec(memory_space=pltpu.HBM)
     smem = pl.BlockSpec(memory_space=pltpu.SMEM)
     dma = pltpu.SemaphoreType.DMA
-    codes, suffix, pre, enc_bias_grad, dec_bias_grad = pl.pallas_call(
+    act_turned, dec_grad, pre, enc_bias_grad, dec_bias_grad = pl.pallas_call(
         exchange_kernel,
         out_shape=[
-            jax.ShapeDtypeStruct((2 * tokens, block), low),
-            jax.ShapeDtypeStruct((HALF, 2, SUB, width), low),
+            jax.ShapeDtypeStruct((width, tokens), low),
+            jax.ShapeDtypeStruct((block, width), low),
             jax.ShapeDtypeStruct((tokens, block), low),
             jax.ShapeDtypeStruct((1, block), full),
             jax.ShapeDtypeStruct((1, width), full),
@@ -485,8 +487,11 @@
             pltpu.VMEM((tokens, block), low),
             pltpu.VMEM((1, block), full),
             pltpu.VMEM((1, width), full),
+            pltpu.VMEM((width, tokens), low),
+            pltpu.VMEM((block, 2 * tokens), low),
+            pltpu.VMEM((block, width), low),
             dma((7,)),
-            dma((4,)),
+            dma((8,)),
             dma((chunks, HALF)),
             dma((chunks, HALF)),
             dma((chunks + 1,)),
@@ -495,7 +500,7 @@
             dma((chunks, HALF)),
             dma((HALF,)),
             dma((HALF,)),
-            dma((4 + chunks,)),
+            dma((5 + chunks,)),
         ],
         compiler_params=pltpu.CompilerParams(
             collective_id=0, has_side_effects=True, vmem_limit_bytes=60 * 1024 * 1024
@@ -504,7 +509,6 @@
     )(
         activations, encoder, encoder_bias, decoder, decoder_bias, kept_mask, boundaries,
     )
-    suffix = suffix.reshape(2 * tokens, width)
     enc_grad, dec_grad, enc_bias_grad, dec_bias_grad = pl.pallas_call(
         grads_kernel,
         out_shape=[
@@ -513,21 +517,18 @@
             jax.ShapeDtypeStruct((block,), full),
             jax.ShapeDtypeStruct((width,), full),
         ],
-        in_specs=[hbm] * 6,
+        in_specs=[hbm] * 5,
         out_specs=[hbm] * 4,
         scratch_shapes=[
-            pltpu.VMEM((tokens, width), low),
+            pltpu.VMEM((width, tokens), low),
             pltpu.VMEM((tokens, block), low),
-            pltpu.VMEM((2 * tokens, block), low),
-            pltpu.VMEM((2 * tokens, width), low),
             pltpu.VMEM((width, block), low),
-            pltpu.VMEM((block, width), low),
-            dma((4,)),
-            dma((2 + 2 * PARTS,)),
+            dma((2,)),
+            dma((3 + PARTS,)),
         ],
         compiler_params=pltpu.CompilerParams(vmem_limit_bytes=60 * 1024 * 1024),
         name="grads",
-    )(activations, pre, codes, suffix, enc_bias_grad, dec_bias_grad)
+    )(act_turned, pre, dec_grad, enc_bias_grad, dec_bias_grad)
     return enc_grad, enc_bias_grad, dec_grad, dec_bias_grad
 
 

time: 42.6 us -> 95.1 us (2.23)
  Pallas kernels: 41.8 us -> 94.3 us
    pallas_call x1, Pallas kernels: 3.53 us -> 57 us  [kernel_body(): pl.pallas_call(grads_kernel, out_shape=[jax.ShapeDtypeStruct((width, bloc...]
    pallas_call x1, Pallas kernels: 38.3 us -> 37.2 us  [kernel_body(): pl.pallas_call(exchange_kernel, out_shape=[jax.ShapeDtypeStruct((width, t...]
where the time goes in v5:
time: 95.1 us; the launch traced here: 94.9 us
  Pallas kernels  94.3 us (99%)
    pallas_call x1, Pallas kernels, kernel_body(): pl.pallas_call(grads_kernel, out_shape=[jax.ShapeDtypeStruct((width, bloc...  57 us
    pallas_call x1, Pallas kernels, kernel_body(): pl.pallas_call(exchange_kernel, out_shape=[jax.ShapeDtypeStruct((width, t...  37.2 us

profile of v5, /device:TPU:0, one launch (start us, length us, event | category | flops | bytes accessed | tf_op | source)
XLA Modules:
  0.0 94.9 jit_solution(2917220205817604273)
XLA Ops:
  0.6 37.2 %exchange.1 = (bf16[1792,128]{1,0:T(8,128)(2,1)}, bf16[512,1792]{1,0:T(8,128)(2,1)}, bf16[128,512]{1,0:T(8,128)(2,1)}, f32[1,512]{1,0:T(1,128)}, f32[1,1792]{1,0:T(1,128)}) custom-call(bf16[128,1792]{1,0:T(8,128)(2,1)} %act_hbm.1, bf16[1792,512]{1,0:T(8,128)(2,1)} %enc_hbm.1, f32[512]{0:T(512)} %enc_bias_hbm.1, bf16[512,1792]{1,0:T(8,128)(2,1)} %dec_hbm.1, ...), custom_call_target="tpu_custom_call" | custom-call | tf_op jit(solution)/shard_map/exchange/pallas_call | solution.py:454
  37.9 57.0 %grads.1 = (bf16[1792,512]{1,0:T(8,128)(2,1)}, bf16[512,1792]{1,0:T(8,128)(2,1)}, f32[512]{0:T(512)}, f32[1792]{0:T(1024)}) custom-call(bf16[1792,128]{1,0:T(8,128)(2,1)} %get-tuple-element.13.act_hbm, bf16[128,512]{1,0:T(8,128)(2,1)} %get-tuple-element.14.pre_hbm, bf16[512,1792]{1,0:T(8,128)(2,1)} %get-tuple-element.15.dec_grad_in, ...), custom_call_target="tpu_custom_call" | custom-call | tf_op jit(solution)/shard_map/grads/pallas_call | solution.py:512

commit v6 on v5

--- a/solution.py
+++ b/solution.py
@@ -418,26 +418,34 @@
 def grads_kernel(
     act_hbm, pre_hbm, dec_grad_in, enc_bias_in, dec_bias_in,
     enc_out, dec_out, enc_bias_out, dec_bias_out,
-    act, pre, enc_grad, load_sems, store_sems,
+    act, pre, enc_grad, dec_grad, load_sems, store_sems,
 ):
     part = act.shape[0] // PARTS
+    rows_each = dec_grad.shape[0] // PARTS
+    bands = [pl.ds(k * rows_each, rows_each) for k in range(PARTS)]
+    moves = [
+        pltpu.make_async_copy(dec_grad_in.at[band], dec_grad.at[band], load_sems.at[2 + k])
+        for k, band in enumerate(bands)
+    ]
     loads = [
         pltpu.make_async_copy(pre_hbm, pre, load_sems.at[0]),
         pltpu.make_async_copy(act_hbm, act, load_sems.at[1]),
     ]
     stores = [
-        pltpu.make_async_copy(dec_grad_in, dec_out, store_sems.at[0]),
-        pltpu.make_async_copy(enc_bias_in.at[0], enc_bias_out, store_sems.at[1]),
-        pltpu.make_async_copy(dec_bias_in.at[0], dec_bias_out, store_sems.at[2]),
+        pltpu.make_async_copy(enc_bias_in.at[0], enc_bias_out, store_sems.at[0]),
+        pltpu.make_async_copy(dec_bias_in.at[0], dec_bias_out, store_sems.at[1]),
     ]
-    for copy in loads + stores:
+    for copy in loads + moves + stores:
         copy.start()
     for load in loads:
         load.wait()
     for k in range(PARTS):
         span, view = slice(k * part, (k + 1) * part), pl.ds(k * part, part)
         enc_grad[span, :] = jnp.dot(act[span, :], pre[...], preferred_element_type=jnp.float32).astype(jnp.bfloat16)
-        stores.append(pltpu.make_async_copy(enc_grad.at[view, :], enc_out.at[view, :], store_sems.at[3 + k]))
+        stores.append(pltpu.make_async_copy(enc_grad.at[view, :], enc_out.at[view, :], store_sems.at[2 + k]))
+        stores[-1].start()
+        moves[k].wait()
+        stores.append(pltpu.make_async_copy(dec_grad.at[bands[k]], dec_out.at[bands[k]], store_sems.at[2 + PARTS + k]))
         stores[-1].start()
     for store in stores:
         store.wait()
@@ -523,8 +531,9 @@
             pltpu.VMEM((width, tokens), low),
             pltpu.VMEM((tokens, block), low),
             pltpu.VMEM((width, block), low),
-            dma((2,)),
-            dma((3 + PARTS,)),
+            pltpu.VMEM((block, width), low),
+            dma((2 + PARTS,)),
+            dma((2 + 2 * PARTS,)),
         ],
         compiler_params=pltpu.CompilerParams(vmem_limit_bytes=60 * 1024 * 1024),
         name="grads",

time: 95.1 us -> 41.4 us (0.44)
  Pallas kernels: 94.3 us -> 40.6 us
    pallas_call x1, Pallas kernels: 57 us -> 3.39 us  [kernel_body(): pl.pallas_call(grads_kernel, out_shape=[jax.ShapeDtypeStruct((width, bloc...]
where the time goes in v6:
time: 41.4 us; the launch traced here: 41.3 us
  Pallas kernels  40.6 us (98%)
  between operations  0.64 us (2%)
    pallas_call x1, Pallas kernels, kernel_body(): pl.pallas_call(exchange_kernel, out_shape=[jax.ShapeDtypeStruct((width, t...  37.2 us
    pallas_call x1, Pallas kernels, kernel_body(): pl.pallas_call(grads_kernel, out_shape=[jax.ShapeDtypeStruct((width, bloc...  3.39 us

profile of v6, /device:TPU:0, one launch (start us, length us, event | category | flops | bytes accessed | tf_op | source)
XLA Modules:
  0.0 41.3 jit_solution(10430793635760877124)
XLA Ops:
  0.6 37.2 %exchange.1 = (bf16[1792,128]{1,0:T(8,128)(2,1)}, bf16[512,1792]{1,0:T(8,128)(2,1)}, bf16[128,512]{1,0:T(8,128)(2,1)}, f32[1,512]{1,0:T(1,128)}, f32[1,1792]{1,0:T(1,128)}) custom-call(bf16[128,1792]{1,0:T(8,128)(2,1)} %act_hbm.1, bf16[1792,512]{1,0:T(8,128)(2,1)} %enc_hbm.1, f32[512]{0:T(512)} %enc_bias_hbm.1, bf16[512,1792]{1,0:T(8,128)(2,1)} %dec_hbm.1, ...), custom_call_target="tpu_custom_call" | custom-call | tf_op jit(solution)/shard_map/exchange/pallas_call | solution.py:462
  37.9 3.4 %grads.1 = (bf16[1792,512]{1,0:T(8,128)(2,1)}, bf16[512,1792]{1,0:T(8,128)(2,1)}, f32[512]{0:T(512)}, f32[1792]{0:T(1024)}) custom-call(bf16[1792,128]{1,0:T(8,128)(2,1)} %get-tuple-element.13.act_hbm, bf16[128,512]{1,0:T(8,128)(2,1)} %get-tuple-element.14.pre_hbm, bf16[512,1792]{1,0:T(8,128)(2,1)} %get-tuple-element.15.dec_grad_in, ...), custom_call_target="tpu_custom_call" | custom-call | tf_op jit(solution)/shard_map/grads/pallas_call | solution.py:520

commit v7 on v6

--- a/solution.py
+++ b/solution.py
@@ -418,7 +418,7 @@
 def grads_kernel(
     act_hbm, pre_hbm, dec_grad_in, enc_bias_in, dec_bias_in,
     enc_out, dec_out, enc_bias_out, dec_bias_out,
-    act, pre, enc_grad, dec_grad, load_sems, store_sems,
+    act, pre, enc_grad, dec_grad, enc_bias, dec_bias, load_sems, store_sems,
 ):
     part = act.shape[0] // PARTS
     rows_each = dec_grad.shape[0] // PARTS
@@ -431,14 +431,20 @@
         pltpu.make_async_copy(pre_hbm, pre, load_sems.at[0]),
         pltpu.make_async_copy(act_hbm, act, load_sems.at[1]),
     ]
+    biases = [
+        pltpu.make_async_copy(enc_bias_in, enc_bias, load_sems.at[2 + PARTS]),
+        pltpu.make_async_copy(dec_bias_in, dec_bias, load_sems.at[3 + PARTS]),
+    ]
     stores = [
-        pltpu.make_async_copy(enc_bias_in.at[0], enc_bias_out, store_sems.at[0]),
-        pltpu.make_async_copy(dec_bias_in.at[0], dec_bias_out, store_sems.at[1]),
+        pltpu.make_async_copy(enc_bias.at[0], enc_bias_out, store_sems.at[0]),
+        pltpu.make_async_copy(dec_bias.at[0], dec_bias_out, store_sems.at[1]),
     ]
-    for copy in loads + moves + stores:
+    for copy in loads + biases + moves:
         copy.start()
-    for load in loads:
+    for load in loads + biases:
         load.wait()
+    for store in stores:
+        store.start()
     for k in range(PARTS):
         span, view = slice(k * part, (k + 1) * part), pl.ds(k * part, part)
         enc_grad[span, :] = jnp.dot(act[span, :], pre[...], preferred_element_type=jnp.float32).astype(jnp.bfloat16)
@@ -532,7 +538,9 @@
             pltpu.VMEM((tokens, block), low),
             pltpu.VMEM((width, block), low),
             pltpu.VMEM((block, width), low),
-            dma((2 + PARTS,)),
+            pltpu.VMEM((1, block), full),
+            pltpu.VMEM((1, width), full),
+            dma((4 + PARTS,)),
             dma((2 + 2 * PARTS,)),
         ],
         compiler_params=pltpu.CompilerParams(vmem_limit_bytes=60 * 1024 * 1024),

time: 41.4 us -> 41.5 us (level)
  no operation moved by 1% of the time
where the time goes in v7:
time: 41.5 us; the launch traced here: 41.3 us
  Pallas kernels  40.7 us (98%)
  between operations  0.64 us (2%)
    pallas_call x1, Pallas kernels, kernel_body(): pl.pallas_call(exchange_kernel, out_shape=[jax.ShapeDtypeStruct((width, t...  37.2 us
    pallas_call x1, Pallas kernels, kernel_body(): pl.pallas_call(grads_kernel, out_shape=[jax.ShapeDtypeStruct((width, bloc...  3.42 us

profile of v7, /device:TPU:0, one launch (start us, length us, event | category | flops | bytes accessed | tf_op | source)
XLA Modules:
  0.0 41.3 jit_solution(4716941480589993190)
XLA Ops:
  0.6 37.2 %exchange.1 = (bf16[1792,128]{1,0:T(8,128)(2,1)}, bf16[512,1792]{1,0:T(8,128)(2,1)}, bf16[128,512]{1,0:T(8,128)(2,1)}, f32[1,512]{1,0:T(1,128)}, f32[1,1792]{1,0:T(1,128)}) custom-call(bf16[128,1792]{1,0:T(8,128)(2,1)} %act_hbm.1, bf16[1792,512]{1,0:T(8,128)(2,1)} %enc_hbm.1, f32[512]{0:T(512)} %enc_bias_hbm.1, bf16[512,1792]{1,0:T(8,128)(2,1)} %dec_hbm.1, ...), custom_call_target="tpu_custom_call" | custom-call | tf_op jit(solution)/shard_map/exchange/pallas_call | solution.py:468
  37.9 3.4 %grads.1 = (bf16[1792,512]{1,0:T(8,128)(2,1)}, bf16[512,1792]{1,0:T(8,128)(2,1)}, f32[512]{0:T(512)}, f32[1792]{0:T(1024)}) custom-call(bf16[1792,128]{1,0:T(8,128)(2,1)} %get-tuple-element.13.act_hbm, bf16[128,512]{1,0:T(8,128)(2,1)} %get-tuple-element.14.pre_hbm, bf16[512,1792]{1,0:T(8,128)(2,1)} %get-tuple-element.15.dec_grad_in, ...), custom_call_target="tpu_custom_call" | custom-call | tf_op jit(solution)/shard_map/grads/pallas_call | solution.py:526
